TPU v7x, 512 devices: a whole 4x4x16 slice. The times are simulated.
512 devices in a mesh: tm: 32 (over z, core), space: 16 (over x, y).
Axes of the slice: x: 4, y: 4, z: 16, core: 2. Of those that a mesh axis runs over, the one named last changes fastest.
Arguments:
- queries: bfloat16 [32, 4096, 2048], P('tm', 'space'), may hold values from -30 to 30
- keys: bfloat16 [32, 4096, 2048], P('tm', 'space'), may hold values from -30 to 30
- values: bfloat16 [32, 4096, 2048], P('tm', 'space'), may hold values from -6 to 6
- groups: int32 [32, 4096], P('tm', 'space'), may hold values from 0 to 511, as said below
Outputs:
- attended: bfloat16 [32, 4096, 2048], P('tm', 'space')
Inputs may be any that keep to these rules, and one draw needn't show every extreme that they name: `groups`: each of the 512 group numbers is held by exactly 256 tokens.
All inputs are finite; a program needn't handle non-finite values.
Results may differ from a plain program's by a relative error of at most 0.012.
Values may be sent and summed in bfloat16 or wider, within the bound.
No kernel may reach another device: no remote copies, remote signals or barrier semaphores. Data moves between devices by JAX's collectives and lax.ppermute only.
A program may use at most 128 MiB of HBM per device.

v0:
```python
import math

import jax
import jax.numpy as jnp
from jax import lax
from jax.sharding import PartitionSpec as P

HEAD_DIM = 128
LANDMARKS = 512
ITERS = 3


def softmax_rows(logits):
    ceiling = jnp.max(logits, axis=-1, keepdims=True)
    expo = jnp.exp(logits - ceiling)
    return expo / jnp.sum(expo, axis=-1, keepdims=True)


def batch_product(left, right):
    return jnp.einsum("hij,hjk->hik", left, right, precision=lax.Precision.HIGHEST)


def frame_attention(pieces):
    q_block, k_block, v_block = pieces
    scale = 1.0 / math.sqrt(q_block.shape[-1])
    logits = (
        jnp.einsum("fphe,gphe->phfg", q_block, k_block, preferred_element_type=jnp.float32) * scale
    )
    weights = softmax_rows(logits).astype(jnp.bfloat16)
    mixed = jnp.einsum("phfg,gphe->fphe", weights, v_block, preferred_element_type=jnp.float32)
    return lax.all_to_all(mixed.astype(jnp.bfloat16), "tm", split_axis=0, concat_axis=1, tiled=True)


def temporal_pass(q_side, k_side, v_side):
    return frame_attention(
        (
            lax.all_to_all(q_side, "tm", split_axis=1, concat_axis=0, tiled=True),
            lax.all_to_all(k_side, "tm", split_axis=1, concat_axis=0, tiled=True),
            lax.all_to_all(v_side, "tm", split_axis=1, concat_axis=0, tiled=True),
        )
    )


def newton_step(own, product):
    first = batch_product(own, product)
    second = batch_product(first, product)
    third = batch_product(second, product)
    return 0.25 * (13.0 * own - 15.0 * first + 7.0 * second - third)


def local(queries, keys, values, groups):
    frames, count, width = queries.shape
    heads = width // HEAD_DIM
    scale = 1.0 / math.sqrt(HEAD_DIM)
    q_four = queries.reshape(frames, count, heads, HEAD_DIM)
    k_four = keys.reshape(frames, count, heads, HEAD_DIM)
    v_four = values.reshape(frames, count, heads, HEAD_DIM)
    temporal = temporal_pass(q_four, k_four, v_four)
    q_heads, k_heads, t_heads = (
        lax.all_to_all(q_four, "space", split_axis=2, concat_axis=1, tiled=True),
        lax.all_to_all(k_four, "space", split_axis=2, concat_axis=1, tiled=True),
        lax.all_to_all(temporal, "space", split_axis=2, concat_axis=1, tiled=True),
    )
    member = lax.all_gather(groups, "space", axis=1, tiled=True)[0]
    q_rows = q_heads[0]
    k_rows = k_heads[0]
    t_rows = t_heads[0]
    landmark_ids = jnp.arange(LANDMARKS, dtype=jnp.int32)
    onehot = (member[None, :] == landmark_ids[:, None]).astype(jnp.bfloat16)
    q_part = jnp.einsum("ms,she->hme", onehot, q_rows, preferred_element_type=jnp.float32)
    k_part = jnp.einsum("ms,she->hme", onehot, k_rows, preferred_element_type=jnp.float32)
    q_total, k_total = lax.psum((q_part, k_part), "tm")
    members_each = lax.axis_size("tm") * q_heads.shape[0] * q_heads.shape[1] // LANDMARKS
    q_land = (q_total / members_each).astype(jnp.bfloat16)
    k_land = (k_total / members_each).astype(jnp.bfloat16)
    kernel = softmax_rows(
        jnp.einsum("hme,hne->hmn", q_land, k_land, preferred_element_type=jnp.float32) * scale
    )
    column_top = jnp.max(jnp.sum(kernel, axis=1), axis=-1)
    iterate = jnp.swapaxes(kernel, 1, 2) / column_top[:, None, None]
    for step in range(ITERS):
        product = batch_product(kernel, iterate)
        iterate = newton_step(iterate, product)
    land_logits = (
        jnp.einsum("hme,she->hms", q_land, k_rows, preferred_element_type=jnp.float32) * scale
    )
    frame_top = jnp.max(land_logits, axis=-1)
    frame_weights = jnp.exp(land_logits - frame_top[..., None])
    frame_total = jnp.sum(frame_weights, axis=-1)
    frame_sum = jnp.einsum(
        "hms,she->hme",
        frame_weights.astype(jnp.bfloat16),
        t_rows,
        preferred_element_type=jnp.float32,
    )
    top = lax.pmax(frame_top, "tm")
    factor = jnp.exp(frame_top - top)
    total, weighted = (
        lax.psum((frame_total * factor).astype(jnp.bfloat16), "tm").astype(jnp.float32),
        lax.psum((frame_sum * factor[..., None]).astype(jnp.bfloat16), "tm").astype(jnp.float32),
    )
    summary = weighted / total[..., None]
    mixed = batch_product(iterate, summary).astype(jnp.bfloat16)
    token_logits = (
        jnp.einsum("she,hme->hsm", q_rows, k_land, preferred_element_type=jnp.float32) * scale
    )
    attend = softmax_rows(token_logits).astype(jnp.bfloat16)
    global_part = jnp.einsum("hsm,hme->she", attend, mixed, preferred_element_type=jnp.float32)
    combined = (t_rows.astype(jnp.float32) + global_part).astype(jnp.bfloat16)[None]
    returned = lax.all_to_all(combined, "space", split_axis=1, concat_axis=2, tiled=True)
    return returned.reshape(frames, count, width)


def solution(mesh):
    return jax.shard_map(
        local,
        mesh=mesh,
        in_specs=(
            P("tm", "space", None),
            P("tm", "space", None),
            P("tm", "space", None),
            P("tm", "space"),
        ),
        out_specs=P("tm", "space", None),
        check_vma=False,
    )
```

profile of v0, /device:TPU:1, one launch (start us, length us, event | category | flops | bytes accessed | tf_op | source)
XLA Modules:
  0.0 843.9 jit_solution(13150337256094075462)
XLA Ops:
  9.3 7.8 all-to-all-start.5
  21.0 7.9 all-to-all-done.5
  28.8 20.2 %all_to_all.108 = bf16[1,256,16,128]{3,1,0,2:T(8,128)(2,1)S(1)} all-to-all(bf16[1,256,16,128]{3,1,0,2:T(8,128)(2,1)S(1)} %copy.70), channel_id=1, replica_groups=mesh['tm'=32,'space'=16] {'space'}, dimensions={2} | all-to-all | bytes 2097152 | tf_op jit(solution)/shard_map/all_to_all | solution.py:61
  49.0 76.2 %all_to_all.109 = bf16[1,256,16,128]{3,2,0,1:T(8,128)(2,1)} all-to-all(bf16[1,256,16,128]{3,2,0,1:T(8,128)(2,1)S(1)} %bitcast.175), channel_id=1, replica_groups=mesh['tm'=32,'space'=16] {'tm'}, dimensions={1} | all-to-all | bytes 2097152 | tf_op jit(solution)/shard_map/all_to_all | solution.py:37
  125.3 4.1 all-to-all-start.1
  131.9 53.3 %all-to-all-done.1 = bf16[1,256,16,128]{3,2,0,1:T(8,128)(2,1)S(1)} async-done(((bf16[1,256,16,128]{3,2,0,1:T(8,128)(2,1)}), bf16[1,256,16,128]{3,2,0,1:T(8,128)(2,1)S(1)}, u32[]{:S(2)}, u32[]{:S(2)}) %all-to-all-start.1) | async-done | bytes 1048608 | tf_op jit(solution)/shard_map/all_to_all | solution.py:38
  185.2 5.3 all-to-all-start.2
  190.5 18.5 %all_gather.3 = s32[1,4096]{1,0:T(1,128)S(1)} all-gather(s32[1,256]{1,0:T(1,128)S(1)} %copy-done.8), channel_id=1, replica_groups=mesh['tm'=32,'space'=16] {'space'}, dimensions={1}, use_global_device_ids=true | all-gather | bytes 17408 | tf_op jit(solution)/shard_map/all_gather | solution.py:64
  209.0 3.3 fusion.20
  214.5 210.6 %all-reduce.6.cloned.1.call-done = (f32[1,512,128]{2,1,0:T(8,128)}, f32[1,512,128]{2,1,0:T(8,128)}) async-done(((f32[1,512,128]{2,1,0:T(8,128)}, f32[1,512,128]{2,1,0:T(8,128)}), (f32[1,512,128]{2,1,0:T(8,128)}, f32[1,512,128]{2,1,0:T(8,128)})) %all-reduce.6.cloned.1.call-update) | async-done | bytes 524304 | tf_op jit(solution)/shard_map/psum | solution.py:72
  430.7 4.7 online-softmax
  435.4 4.9 fusion.72
  444.5 11.8 %all-to-all-start.3 = ((bf16[32,8,16,128]{3,2,1,0:T(8,128)(2,1)}), bf16[32,8,16,128]{3,2,1,0:T(8,128)(2,1)}, u32[]{:S(2)}, u32[]{:S(2)}) async-start(bf16[32,8,16,128]{3,2,1,0:T(8,128)(2,1)} %copy.66), calls=%async_computation.3 | async-start | bytes 2097152 | tf_op jit(solution)/shard_map/all_to_all | solution.py:31
  463.2 4.7 online-softmax.1
  467.9 3.1 fusion.70
  471.1 3.1 fusion.80
  474.1 3.4 fusion.16
  478.6 4.7 online-softmax.2
  483.3 5.8 multiply_reduce_fusion.1
  489.0 52.5 %pmax.7 = f32[1,512]{1,0:T(1,128)S(1)} all-reduce(f32[1,512]{1,0:T(1,128)S(1)} %bitcast.187), channel_id=1, replica_groups=mesh['tm'=32,'space'=16] {'tm'}, use_global_device_ids=true, to_apply=%region_9.0 | all-reduce | flops 512 | bytes 4096 | tf_op jit(solution)/shard_map/pmax | solution.py:96
  541.5 4.9 fusion.3
  548.3 2.8 fusion.81
  553.7 6.6 all-to-all-start.4
  562.8 3.2 copy-done
  567.4 7.8 all-to-all-done.4
  575.2 5.7 fusion.28
  580.9 4.5 fusion.19
  585.4 48.5 %psum.31 = bf16[512]{0:T(512)(128)(2,1)S(1)} all-reduce(bf16[512]{0:T(512)(128)(2,1)S(1)} %get-tuple-element.7), channel_id=1, replica_groups=mesh['tm'=32,'space'=16] {'tm'}, use_global_device_ids=true, to_apply=%region_12.0 | all-reduce | flops 512 | bytes 2048 | tf_op jit(solution)/shard_map/psum | solution.py:99
  635.5 142.3 %all-reduce.4.cloned.1.call-done = bf16[1,512,128]{2,1,0:T(8,128)(2,1)} async-done(((bf16[1,512,128]{2,1,0:T(8,128)(2,1)}), bf16[1,512,128]{2,1,0:T(8,128)(2,1)}) %all-reduce.4.cloned.1.call-update) | async-done | bytes 131088 | tf_op jit(solution)/shard_map/psum | solution.py:100
  780.1 5.4 fusion.8
  788.8 22.4 %reduce.20 = bf16[4096,128]{1,0:T(8,128)(2,1)S(1)} reduce(bf16[4096,1,1,128]{3,2,1,0:T(2,128)(2,1)S(1)} %bitcast.177, bf16[]{:T(256)} %broadcast.92), dimensions={1,2}, to_apply=%bitcast.141.reduce_sub_computation | reduce | bytes 2097154
  811.5 22.2 %all_to_all.110 = bf16[16,2,16384]{2,1,0:T(2,128)(2,1)S(1)} all-to-all(bf16[16,2,16384]{2,1,0:T(2,128)(2,1)S(1)} %reshape.227), channel_id=1, replica_groups=mesh['tm'=32,'space'=16] {'space'}, dimensions={0} | all-to-all | bytes 2097152 | tf_op jit(solution)/shard_map/all_to_all | solution.py:110
  (58 shorter events, 47.9 us)
Async XLA Ops:
  9.3 181.3 %copy-start.8 = (s32[1,256]{1,0:T(1,128)S(1)}, s32[1,256]{1,0:T(1,128)}, u32[]{:S(2)}) copy-start(s32[1,256]{1,0:T(1,128)} %param.7) | copy-start | bytes 3076
  9.3 19.6 %all-to-all-start.5 = ((bf16[1,256,16,128]{3,1,0,2:T(8,128)(2,1)}), bf16[1,256,16,128]{3,1,0,2:T(8,128)(2,1)}, u32[]{:S(2)}, u32[]{:S(2)}) async-start(bf16[1,256,16,128]{3,1,0,2:T(8,128)(2,1)} %copy.69), calls=%async_computation.5 | async-start | bytes 2097152 | tf_op jit(solution)/shard_map/all_to_all | solution.py:60
  49.0 165.4 %copy-start.4 = (bf16[1,256,16,128]{3,1,0,2:T(8,128)(2,1)}, bf16[1,256,16,128]{3,1,0,2:T(8,128)(2,1)S(1)}, u32[]{:S(2)}) copy-start(bf16[1,256,16,128]{3,1,0,2:T(8,128)(2,1)S(1)} %all_to_all.108) | copy-start | bytes 3145732
  125.3 59.9 %all-to-all-start.1 = ((bf16[1,256,16,128]{3,2,0,1:T(8,128)(2,1)}), bf16[1,256,16,128]{3,2,0,1:T(8,128)(2,1)S(1)}, u32[]{:S(2)}, u32[]{:S(2)}) async-start(bf16[1,256,16,128]{3,2,0,1:T(8,128)(2,1)} %bitcast.75), calls=%async_computation.1 | async-start | bytes 2097152 | tf_op jit(solution)/shard_map/all_to_all | solution.py:38
  185.2 242.9 %copy-start.7 = (bf16[1,256,16,128]{3,2,0,1:T(8,128)(2,1)}, bf16[1,256,16,128]{3,2,0,1:T(8,128)(2,1)S(1)}, u32[]{:S(2)}) copy-start(bf16[1,256,16,128]{3,2,0,1:T(8,128)(2,1)S(1)} %all-to-all-done.1) | copy-start | bytes 3145732
  185.2 255.1 %all-to-all-start.2 = ((bf16[1,256,16,128]{3,2,0,1:T(8,128)(2,1)}), bf16[1,256,16,128]{3,2,0,1:T(8,128)(2,1)}, u32[]{:S(2)}, u32[]{:S(2)}) async-start(bf16[1,256,16,128]{3,2,0,1:T(8,128)(2,1)} %bitcast.80), calls=%async_computation.2 | async-start | bytes 2097152 | tf_op jit(solution)/shard_map/all_to_all | solution.py:39
  190.5 234.5 %all-reduce.6.cloned.1.call-start = ((), (), s32[]{:S(2)}) async-start(), calls=%async_computation.9 | async-start | bytes 1048576 | tf_op jit(solution)/shard_map/psum | solution.py:72
  435.4 20.9 %copy-start.2 = (f32[512,512]{1,0:T(8,128)S(1)}, f32[512,512]{1,0:T(8,128)}, u32[]{:S(2)}) copy-start(f32[512,512]{1,0:T(8,128)} %online-softmax) | copy-start | bytes 3145732
  435.4 20.9 %copy-start.3 = (f32[512,512]{1,0:T(8,128)S(1)}, f32[512,512]{1,0:T(8,128)}, u32[]{:S(2)}) copy-start(f32[512,512]{1,0:T(8,128)} %fusion.39) | copy-start | bytes 3145732
  444.5 106.7 %all-to-all-start.3 = ((bf16[32,8,16,128]{3,2,1,0:T(8,128)(2,1)}), bf16[32,8,16,128]{3,2,1,0:T(8,128)(2,1)}, u32[]{:S(2)}, u32[]{:S(2)}) async-start(bf16[32,8,16,128]{3,2,1,0:T(8,128)(2,1)} %copy.66), calls=%async_computation.3 | async-start | bytes 2097152 | tf_op jit(solution)/shard_map/all_to_all | solution.py:31
  467.9 15.3 %copy-start.6 = (f32[1,512,128]{2,1,0:T(8,128)S(1)}, f32[1,512,128]{2,1,0:T(8,128)}, u32[]{:S(2)}) copy-start(f32[1,512,128]{2,1,0:T(8,128)} %get-tuple-element.6) | copy-start | bytes 786436
  483.2 63.2 %copy-start.1 = (f32[512,512]{1,0:T(8,128)S(1)}, f32[512,512]{1,0:T(8,128)}, u32[]{:S(2)}) copy-start(f32[512,512]{1,0:T(8,128)} %online-softmax.2) | copy-start | bytes 3145732
  541.5 18.8 %copy-start.5 = (f32[1,512,128]{2,1,0:T(8,128)S(1)}, f32[1,512,128]{2,1,0:T(8,128)}, u32[]{:S(2)}) copy-start(f32[1,512,128]{2,1,0:T(8,128)} %get-tuple-element.5) | copy-start | bytes 786436
  553.7 21.6 %all-to-all-start.4 = ((bf16[1,256,16,128]{3,1,0,2:T(8,128)(2,1)}), bf16[1,256,16,128]{3,1,0,2:T(8,128)(2,1)}, u32[]{:S(2)}, u32[]{:S(2)}) async-start(bf16[1,256,16,128]{3,1,0,2:T(8,128)(2,1)} %copy.67), calls=%async_computation.4 | async-start | bytes 2097152 | tf_op jit(solution)/shard_map/all_to_all | solution.py:62
  560.2 217.5 %all-reduce.4.cloned.1.call-start = ((), (), s32[]{:S(2)}) async-start(), calls=%async_computation.8 | async-start | bytes 262144 | tf_op jit(solution)/shard_map/psum | solution.py:100
  562.8 3.2 copy-start
Sparse Core Ops, SparseCore 0:
  214.6 210.3 all-reduce.5
  581.1 196.6 all-reduce.3
where the time goes:
time: 848 us; the launch traced here: 844 us
  waiting for transfers between devices  422 us (50%)
  blocking collectives  238 us (28%)
  matrix products  60.7 us (7%)
  starting transfers between devices  35.6 us (4%)
  other arithmetic  33.9 us (4%)
  local copies, waits for them, and re-layouts  25.8 us (3%)
  Pallas kernels  14.1 us (2%)
  between operations  13.9 us (2%)
    psum x1, waiting for transfers between devices, local(): q_total, k_total = lax.psum((q_part, k_part), 'tm')  211 us
    psum x1, waiting for transfers between devices, local(): lax.psum((frame_sum * factor[..., None]).astype(jnp.bfloat16), 'tm')  142 us
    all_to_all x1, blocking collectives, temporal_pass(): lax.all_to_all(q_side, 'tm', split_axis=1, concat_axis=0, tiled=True)  76.2 us
    all_to_all x1, waiting for transfers between devices, temporal_pass(): lax.all_to_all(k_side, 'tm', split_axis=1, concat_axis=0, tiled=True)  53.3 us
    pmax x1, blocking collectives, local(): top = lax.pmax(frame_top, 'tm')  52.5 us
    psum x1, blocking collectives, local(): lax.psum((frame_total * factor).astype(jnp.bfloat16), 'tm')  48.5 us
    dot_general x10, matrix products, batch_product(): jnp.einsum('hij,hjk->hik', left, right, precision=lax.Precision.HIGHEST)  26.8 us
    unnamed x1, other arithmetic  22.4 us
  transfers between devices with their start and end apart: 7, of which 5 were waited for; matrix products, arithmetic and copies ran while one was open for 8% of the time, Pallas kernels for 2%

commit v1 on v0

v1 whole, which is shorter than its diff:
```python
import math

import jax
import jax.numpy as jnp
from jax import lax
from jax.sharding import PartitionSpec as P

HEAD_DIM = 128
LANDMARKS = 512
ITERS = 3
BOTH = ("tm", "space")


def softmax_rows(logits):
    ceiling = jnp.max(logits, axis=-1, keepdims=True)
    expo = jnp.exp(logits - ceiling)
    return expo / jnp.sum(expo, axis=-1, keepdims=True)


def product(left, right):
    return jnp.dot(left, right, precision=lax.Precision.HIGHEST)


def swap(x, axes):
    return lax.all_to_all(x, axes, split_axis=0, concat_axis=0, tiled=True)


def share(x, axis):
    size = lax.axis_size(axis)
    return swap(jnp.broadcast_to(x[None], (size,) + x.shape), axis)


def total_over(x):
    size = lax.axis_size("tm")
    rows, width = x.shape
    parts = swap(x.astype(jnp.bfloat16).reshape(size, rows // size, width), "tm")
    return jnp.sum(parts.astype(jnp.float32), axis=0)


def local(queries, keys, values, groups):
    frames, count, width = queries.shape
    heads = width // HEAD_DIM
    scale = 1.0 / math.sqrt(HEAD_DIM)
    tm, space = lax.axis_size("tm"), lax.axis_size("space")
    few = count // tm

    def tiles(x):
        x = x.reshape(tm, few, heads, HEAD_DIM)
        return jnp.swapaxes(x, 1, 2).reshape(tm * heads, few, HEAD_DIM)

    qk = jnp.stack([tiles(queries), tiles(keys)], axis=1)
    qk = swap(qk, BOTH)
    v = swap(tiles(values), BOTH)
    member = swap(groups.reshape(tm, few), "tm")
    member = lax.all_gather(member, "space")
    member = jnp.swapaxes(member, 0, 1).reshape(-1)

    tokens = tm * space * few
    q = qk[:, 0].reshape(tokens, HEAD_DIM)
    k = qk[:, 1].reshape(tokens, HEAD_DIM)
    v = v.reshape(tokens, HEAD_DIM)

    landmark_ids = jnp.arange(LANDMARKS, dtype=jnp.int32)
    onehot = (member[None, :] == landmark_ids[:, None]).astype(jnp.bfloat16)
    q_part = jnp.dot(onehot, q, preferred_element_type=jnp.float32)
    k_part = jnp.dot(onehot, k, preferred_element_type=jnp.float32)
    block = LANDMARKS // tm
    both = jnp.concatenate(
        [q_part.reshape(tm, block, HEAD_DIM), k_part.reshape(tm, block, HEAD_DIM)], axis=1
    )
    sums = total_over(both.reshape(2 * LANDMARKS, HEAD_DIM))
    members_each = tm * tokens // LANDMARKS
    lands = share((sums / members_each).astype(jnp.bfloat16), "tm")
    q_land = lands[:, :block].reshape(LANDMARKS, HEAD_DIM)
    k_land = lands[:, block:].reshape(LANDMARKS, HEAD_DIM)

    def split(x):
        x = x.reshape(tm, space, few, HEAD_DIM)
        return jnp.swapaxes(x, 0, 1).reshape(space, tm * few, HEAD_DIM)

    qs, ks, vs = split(q), split(k), split(v)
    logits = jnp.einsum("sae,sbe->sab", qs, ks, preferred_element_type=jnp.float32) * scale
    index = jnp.arange(tm * few, dtype=jnp.int32) % few
    logits = jnp.where(index[:, None] == index[None, :], logits, -jnp.inf)
    weights = softmax_rows(logits).astype(jnp.bfloat16)
    temporal = jnp.einsum("sab,sbe->sae", weights, vs, preferred_element_type=jnp.float32)
    temporal = temporal.astype(jnp.bfloat16).reshape(space, tm, few, HEAD_DIM)
    temporal = jnp.swapaxes(temporal, 0, 1).reshape(tokens, HEAD_DIM)

    kernel = softmax_rows(
        jnp.einsum("me,ne->mn", q_land, k_land, preferred_element_type=jnp.float32) * scale
    )
    column_top = jnp.max(jnp.sum(kernel, axis=0))
    iterate = kernel.T / column_top
    for step in range(ITERS):
        gain = product(kernel, iterate)
        first = product(iterate, gain)
        second = product(first, gain)
        third = product(second, gain)
        iterate = 0.25 * (13.0 * iterate - 15.0 * first + 7.0 * second - third)

    land_logits = jnp.einsum("me,se->ms", q_land, k, preferred_element_type=jnp.float32) * scale
    own_top = jnp.max(land_logits, axis=-1)
    own_weights = jnp.exp(land_logits - own_top[:, None])
    own_total = jnp.sum(own_weights, axis=-1)
    pair = share(jnp.stack([own_top, own_total]).reshape(-1, 128), "tm")
    pair = pair.reshape(tm, 2, LANDMARKS)
    top = jnp.max(pair[:, 0], axis=0)
    total = jnp.sum(pair[:, 1] * jnp.exp(pair[:, 0] - top), axis=0)
    own_sum = jnp.dot(own_weights.astype(jnp.bfloat16), temporal, preferred_element_type=jnp.float32)
    share_of = jnp.exp(own_top - top) / total
    summary = total_over(own_sum * share_of[:, None])
    summary = share(summary.astype(jnp.bfloat16), "tm").reshape(LANDMARKS, HEAD_DIM)
    mixed = product(iterate, summary.astype(jnp.float32)).astype(jnp.bfloat16)

    token_logits = jnp.einsum("se,me->sm", q, k_land, preferred_element_type=jnp.float32) * scale
    attend = softmax_rows(token_logits).astype(jnp.bfloat16)
    global_part = jnp.dot(attend, mixed, preferred_element_type=jnp.float32)
    combined = (temporal.astype(jnp.float32) + global_part).astype(jnp.bfloat16)
    back = swap(combined.reshape(tm * space, few, HEAD_DIM), BOTH)
    back = jnp.swapaxes(back.reshape(tm, heads, few, HEAD_DIM), 1, 2)
    return back.reshape(frames, count, width)


def solution(mesh):
    return jax.shard_map(
        local,
        mesh=mesh,
        in_specs=(
            P("tm", "space", None),
            P("tm", "space", None),
            P("tm", "space", None),
            P("tm", "space"),
        ),
        out_specs=P("tm", "space", None),
        check_vma=False,
    )
```

time: 848 us -> 457 us (0.54)
  waiting for transfers between devices: 422 us -> 175 us
  blocking collectives: 238 us -> 115 us
  starting transfers between devices: 35.6 us -> 65.4 us
  other arithmetic: 33.9 us -> 15 us
  local copies, waits for them, and re-layouts: 25.8 us -> 11 us
  between operations: 13.9 us -> 0.44 us
  matrix products: 60.7 us -> 49.9 us
    psum x2 -> x0, waiting for transfers between devices: 353 us -> none  [the longest x1 211 us: local(): q_total, k_total = lax.psum((q_part, k_part), 'tm')]
    all_to_all x5 -> x7, waiting for transfers between devices: 69 us -> 175 us  [swap(): return lax.all_to_all(x, axes, split_axis=0, concat_axis=0, tiled=True)]
    pmax x1 -> x0, blocking collectives: 52.5 us -> none  [local(): top = lax.pmax(frame_top, 'tm')]
    psum x1 -> x0, blocking collectives: 48.5 us -> none  [local(): lax.psum((frame_total * factor).astype(jnp.bfloat16), 'tm')]
    all_to_all x5 -> x7, starting transfers between devices: 35.5 us -> 65.4 us  [swap(): return lax.all_to_all(x, axes, split_axis=0, concat_axis=0, tiled=True)]
    all_to_all x3 -> x2, blocking collectives: 119 us -> 94.4 us  [swap(): return lax.all_to_all(x, axes, split_axis=0, concat_axis=0, tiled=True)]
    unnamed x1, other arithmetic: 22.4 us -> 1.34 us
    dot_general x18 -> x19, matrix products: 55.8 us -> 49.9 us  [the longest x11 32 us: product(): return jnp.dot(left, right, precision=lax.Precision.HIGHEST)]
  transfers between devices with their start and end apart: 7 -> 7, of which waited for: 5 -> 6; matrix products, arithmetic and copies ran while one was open for 8% -> 12% of each run, Pallas kernels for 2% -> 2%
where the time goes in v1:
time: 457 us; the launch traced here: 448 us
  waiting for transfers between devices  175 us (38%)
  blocking collectives  115 us (25%)
  starting transfers between devices  65.4 us (14%)
  matrix products  49.9 us (11%)
  Pallas kernels  17.2 us (4%)
  other arithmetic  15 us (3%)
  local copies, waits for them, and re-layouts  11 us (2%)
    all_to_all x7, waiting for transfers between devices, swap(): return lax.all_to_all(x, axes, split_axis=0, concat_axis=0, tiled=True)  175 us
    all_to_all x2, blocking collectives, swap(): return lax.all_to_all(x, axes, split_axis=0, concat_axis=0, tiled=True)  94.4 us
    all_to_all x7, starting transfers between devices, swap(): return lax.all_to_all(x, axes, split_axis=0, concat_axis=0, tiled=True)  65.4 us
    dot_general x11, matrix products, product(): return jnp.dot(left, right, precision=lax.Precision.HIGHEST)  32 us
    all_gather x1, blocking collectives, local(): member = lax.all_gather(member, 'space')  20.3 us
    unnamed x3, Pallas kernels  17.2 us
  transfers between devices with their start and end apart: 7, of which 6 were waited for; matrix products, arithmetic and copies ran while one was open for 12% of the time, Pallas kernels for 2%

profile of v1, /device:TPU:1, one launch (start us, length us, event | category | flops | bytes accessed | tf_op | source)
XLA Modules:
  0.0 448.4 jit_solution(9569818378988820790)
XLA Ops:
  2.6 16.8 %all-to-all-start.2 = ((s32[32,1,8]{2,1,0:T(1,128)}), s32[32,1,8]{2,1,0:T(1,128)S(1)}, u32[]{:S(2)}, u32[]{:S(2)}) async-start(s32[32,1,8]{2,1,0:T(1,128)} %bitcast.22), calls=%async_computation.2 | async-start | bytes 32768 | tf_op jit(solution)/shard_map/all_to_all | solution.py:25
  19.3 3.2 pad_maximum_fusion
  22.5 8.5 %all-to-all-done.2 = s32[32,1,8]{2,1,0:T(1,128)S(1)} async-done(((s32[32,1,8]{2,1,0:T(1,128)}), s32[32,1,8]{2,1,0:T(1,128)S(1)}, u32[]{:S(2)}, u32[]{:S(2)}) %all-to-all-start.2) | async-done | bytes 1056 | tf_op jit(solution)/shard_map/all_to_all | solution.py:25
  31.0 11.3 %all-to-all-start = ((bf16[512,2,8,128]{3,2,1,0:T(8,128)(2,1)}), bf16[512,2,8,128]{3,2,1,0:T(8,128)(2,1)S(1)}, u32[]{:S(2)}, u32[]{:S(2)}) async-start(bf16[512,2,8,128]{3,2,1,0:T(8,128)(2,1)} %pad_maximum_fusion), calls=%async_computation | async-start | bytes 4194304 | tf_op jit(solution)/shard_map/all_to_all | solution.py:25
  42.3 20.3 %all-gather = s32[512,1,8]{2,1,0:T(1,128)S(1)} all-gather(s32[32,1,8]{2,1,0:T(1,128)S(1)} %all-to-all-done.2), channel_id=2, replica_groups=mesh['tm'=32,'space'=16] {'space'}, dimensions={0}, use_global_device_ids=true | all-gather | bytes 17408 | tf_op jit(solution)/shard_map/all_gather | solution.py:55
  62.9 81.1 %all-to-all-done = bf16[512,2,8,128]{3,2,1,0:T(8,128)(2,1)S(1)} async-done(((bf16[512,2,8,128]{3,2,1,0:T(8,128)(2,1)}), bf16[512,2,8,128]{3,2,1,0:T(8,128)(2,1)S(1)}, u32[]{:S(2)}, u32[]{:S(2)}) %all-to-all-start) | async-done | bytes 2097184 | tf_op jit(solution)/shard_map/all_to_all | solution.py:25
  146.7 26.6 %all_to_all.49 = bf16[32,32,128]{2,1,0:T(8,128)(2,1)S(1)} all-to-all(bf16[32,32,128]{2,1,0:T(8,128)(2,1)S(1)} %pad_maximum_fusion.1), channel_id=1, replica_groups=mesh['tm'=32,'space'=16] {'tm'}, dimensions={0} | all-to-all | bytes 524288 | tf_op jit(solution)/shard_map/all_to_all | solution.py:25
  173.3 9.2 %all-to-all-start.1 = ((bf16[512,8,128]{2,1,0:T(8,128)(2,1)}), bf16[512,8,128]{2,1,0:T(8,128)(2,1)S(1)}, u32[]{:S(2)}, u32[]{:S(2)}) async-start(bf16[512,8,128]{2,1,0:T(8,128)(2,1)} %bitcast.14), calls=%async_computation.1 | async-start | bytes 2097152 | tf_op jit(solution)/shard_map/all_to_all | solution.py:25
  182.8 2.6 fusion.41
  185.5 54.9 %all-to-all-done.1 = bf16[512,8,128]{2,1,0:T(8,128)(2,1)S(1)} async-done(((bf16[512,8,128]{2,1,0:T(8,128)(2,1)}), bf16[512,8,128]{2,1,0:T(8,128)(2,1)S(1)}, u32[]{:S(2)}, u32[]{:S(2)}) %all-to-all-start.1) | async-done | bytes 1048608 | tf_op jit(solution)/shard_map/all_to_all | solution.py:25
  241.2 5.8 %all-to-all-start.4 = ((bf16[32,32,128]{2,1,0:T(8,128)(2,1)}), bf16[32,32,128]{2,1,0:T(8,128)(2,1)}, u32[]{:S(2)}, u32[]{:S(2)}) async-start(bf16[32,32,128]{2,1,0:T(8,128)(2,1)} %broadcast_in_dim.18), calls=%async_computation.4 | async-start | bytes 524288 | tf_op jit(solution)/shard_map/all_to_all | solution.py:25
  247.0 5.0 %fusion.72 = (f32[16,256]{1,0:T(8,128)S(1)}, f32[16,256,256]{1,2,0:T(8,128)S(1)}) fusion(f32[16,256,256]{1,2,0:T(8,128)} %fusion.41, pred[256,256]{0,1:T(8,128)(4,1)S(1)} %broadcast_compare_fusion), kind=kOutput, calls=%fused_computation.88 | output fusion | flops 6291711 | bytes 8470528 | tf_op jit(solution)/shard_map/sub | solution.py:16
  254.2 14.7 %all-to-all-done.4 = bf16[32,32,128]{2,1,0:T(8,128)(2,1)} async-done(((bf16[32,32,128]{2,1,0:T(8,128)(2,1)}), bf16[32,32,128]{2,1,0:T(8,128)(2,1)}, u32[]{:S(2)}, u32[]{:S(2)}) %all-to-all-start.4) | async-done | bytes 262176 | tf_op jit(solution)/shard_map/all_to_all | solution.py:25
  275.1 4.6 %all-to-all-start.5 = ((f32[32,8,128]{2,1,0:T(8,128)}), f32[32,8,128]{2,1,0:T(8,128)S(1)}, u32[]{:S(2)}, u32[]{:S(2)}) async-start(f32[32,8,128]{2,1,0:T(8,128)} %broadcast_in_dim.20), calls=%async_computation.5 | async-start | bytes 262144 | tf_op jit(solution)/shard_map/all_to_all | solution.py:25
  283.1 2.1 fusion.50
  289.0 3.5 broadcast_multiply_fusion.1
  292.5 4.8 %online-softmax = f32[512,512]{1,0:T(8,128)} custom-call(f32[512,512]{1,0:T(8,128)} %copy.63, f32[512,512]{1,0:T(8,128)} %get-tuple-element.14), custom_call_target="tpu_custom_call" | custom-call | tf_op online-softmax
  297.3 3.9 fusion.60
  301.2 3.1 fusion.74
  304.3 3.3 broadcast_multiply_fusion
  307.5 4.7 %online-softmax.1 = f32[512,512]{1,0:T(8,128)} custom-call(f32[512,512]{1,0:T(8,128)} %copy.63, f32[512,512]{1,0:T(8,128)} %get-tuple-element.16), custom_call_target="tpu_custom_call" | custom-call | tf_op online-softmax
  312.5 5.8 %fusion.24 = bf16[512,128]{1,0:T(8,128)(2,1)} fusion(bf16[4096,128]{1,0:T(8,128)(2,1)} %bitcast.122, f32[512,4096]{1,0:T(8,128)} %copy-done, f32[512]{0:T(512)S(1)} %get-tuple-element.20, f32[512]{0:T(512)S(1)} %exponential_divide_fusion), kind=kOutput, calls=%fused_computation.33 | convolution fusion | flops 543293440 | bytes 9572352 | tf_op jit(solution)/shard_map/dot_general | solution.py:110
  318.3 12.3 %all-to-all-start.6 = ((bf16[32,16,128]{2,1,0:T(8,128)(2,1)}), bf16[32,16,128]{2,1,0:T(8,128)(2,1)S(1)}, u32[]{:S(2)}, u32[]{:S(2)}) async-start(bf16[32,16,128]{2,1,0:T(8,128)(2,1)} %bitcast.35), calls=%async_computation.6 | async-start | bytes 262144 | tf_op jit(solution)/shard_map/all_to_all | solution.py:25
  330.6 3.1 fusion.61
  334.6 2.8 fusion.75
  337.5 9.0 %all-to-all-done.6 = bf16[32,16,128]{2,1,0:T(8,128)(2,1)S(1)} async-done(((bf16[32,16,128]{2,1,0:T(8,128)(2,1)}), bf16[32,16,128]{2,1,0:T(8,128)(2,1)S(1)}, u32[]{:S(2)}, u32[]{:S(2)}) %all-to-all-start.6) | async-done | bytes 131104 | tf_op jit(solution)/shard_map/all_to_all | solution.py:25
  347.1 5.4 %all-to-all-start.7 = ((bf16[32,16,128]{2,1,0:T(8,128)(2,1)}), bf16[32,16,128]{2,1,0:T(8,128)(2,1)S(1)}, u32[]{:S(2)}, u32[]{:S(2)}) async-start(bf16[32,16,128]{2,1,0:T(8,128)(2,1)} %broadcast_in_dim.21), calls=%async_computation.7 | async-start | bytes 262144 | tf_op jit(solution)/shard_map/all_to_all | solution.py:25
  352.5 5.1 %fusion.20 = f32[512,512]{1,0:T(8,128)} fusion(f32[512,512]{1,0:T(8,128)} %fusion.75, f32[512,512]{1,0:T(8,128)S(1)} %copy-done.1, f32[512,512]{1,0:T(8,128)} %copy-done.3, f32[512,512]{1,0:T(8,128)} %get-tuple-element.17), kind=kOutput, calls=%fused_computation.28 | convolution fusion | flops 1612447744 | bytes 5242880 | tf_op jit(solution)/shard_map/dot_general | solution.py:21
  357.7 4.5 convolution_multiply_fusion
  362.1 6.4 %all-to-all-done.7 = bf16[32,16,128]{2,1,0:T(8,128)(2,1)S(1)} async-done(((bf16[32,16,128]{2,1,0:T(8,128)(2,1)}), bf16[32,16,128]{2,1,0:T(8,128)(2,1)S(1)}, u32[]{:S(2)}, u32[]{:S(2)}) %all-to-all-start.7) | async-done | bytes 131104 | tf_op jit(solution)/shard_map/all_to_all | solution.py:25
  369.9 7.8 %online-softmax.2 = f32[4096,128]{1,0:T(8,128)} custom-call(f32[4096,512]{1,0:T(8,128)} %convolution_multiply_fusion, f32[512,128]{1,0:T(8,128)} %fusion.76), custom_call_target="tpu_custom_call" | custom-call | tf_op online-softmax
  379.5 67.8 %all_to_all.50 = bf16[512,8,128]{2,1,0:T(8,128)(2,1)S(1)} all-to-all(bf16[512,8,128]{2,1,0:T(8,128)(2,1)S(1)} %fusion.33), channel_id=1, replica_groups=mesh['tm'=32,'space'=16] {'tm','space'}, dimensions={0} | all-to-all | bytes 2097152 | tf_op jit(solution)/shard_map/all_to_all | solution.py:25
  (55 shorter events, 28.0 us)
Async XLA Ops:
  2.6 28.5 %all-to-all-start.2 = ((s32[32,1,8]{2,1,0:T(1,128)}), s32[32,1,8]{2,1,0:T(1,128)S(1)}, u32[]{:S(2)}, u32[]{:S(2)}) async-start(s32[32,1,8]{2,1,0:T(1,128)} %bitcast.22), calls=%async_computation.2 | async-start | bytes 32768 | tf_op jit(solution)/shard_map/all_to_all | solution.py:25
  31.0 113.0 %all-to-all-start = ((bf16[512,2,8,128]{3,2,1,0:T(8,128)(2,1)}), bf16[512,2,8,128]{3,2,1,0:T(8,128)(2,1)S(1)}, u32[]{:S(2)}, u32[]{:S(2)}) async-start(bf16[512,2,8,128]{3,2,1,0:T(8,128)(2,1)} %pad_maximum_fusion), calls=%async_computation | async-start | bytes 4194304 | tf_op jit(solution)/shard_map/all_to_all | solution.py:25
  173.3 67.2 %all-to-all-start.1 = ((bf16[512,8,128]{2,1,0:T(8,128)(2,1)}), bf16[512,8,128]{2,1,0:T(8,128)(2,1)S(1)}, u32[]{:S(2)}, u32[]{:S(2)}) async-start(bf16[512,8,128]{2,1,0:T(8,128)(2,1)} %bitcast.14), calls=%async_computation.1 | async-start | bytes 2097152 | tf_op jit(solution)/shard_map/all_to_all | solution.py:25
  241.2 27.7 %all-to-all-start.4 = ((bf16[32,32,128]{2,1,0:T(8,128)(2,1)}), bf16[32,32,128]{2,1,0:T(8,128)(2,1)}, u32[]{:S(2)}, u32[]{:S(2)}) async-start(bf16[32,32,128]{2,1,0:T(8,128)(2,1)} %broadcast_in_dim.18), calls=%async_computation.4 | async-start | bytes 524288 | tf_op jit(solution)/shard_map/all_to_all | solution.py:25
  271.2 3.2 copy-start
  275.1 37.1 %all-to-all-start.5 = ((f32[32,8,128]{2,1,0:T(8,128)}), f32[32,8,128]{2,1,0:T(8,128)S(1)}, u32[]{:S(2)}, u32[]{:S(2)}) async-start(f32[32,8,128]{2,1,0:T(8,128)} %broadcast_in_dim.20), calls=%async_computation.5 | async-start | bytes 262144 | tf_op jit(solution)/shard_map/all_to_all | solution.py:25
  292.5 11.7 %copy-start.5 = (f32[512,512]{1,0:T(8,128)S(1)}, f32[512,512]{1,0:T(8,128)}, u32[]{:S(2)}) copy-start(f32[512,512]{1,0:T(8,128)} %get-tuple-element.15) | copy-start | bytes 3145732
  297.3 7.0 %copy-start.2 = (f32[512,512]{1,0:T(8,128)S(1)}, f32[512,512]{1,0:T(8,128)}, u32[]{:S(2)}) copy-start(f32[512,512]{1,0:T(8,128)} %online-softmax) | copy-start | bytes 3145732
  312.5 18.1 %copy-start.1 = (f32[512,512]{1,0:T(8,128)S(1)}, f32[512,512]{1,0:T(8,128)}, u32[]{:S(2)}) copy-start(f32[512,512]{1,0:T(8,128)} %online-softmax.1) | copy-start | bytes 3145732
  318.3 28.1 %all-to-all-start.6 = ((bf16[32,16,128]{2,1,0:T(8,128)(2,1)}), bf16[32,16,128]{2,1,0:T(8,128)(2,1)S(1)}, u32[]{:S(2)}, u32[]{:S(2)}) async-start(bf16[32,16,128]{2,1,0:T(8,128)(2,1)} %bitcast.35), calls=%async_computation.6 | async-start | bytes 262144 | tf_op jit(solution)/shard_map/all_to_all | solution.py:25
  333.7 1.0 copy-start.3
  347.1 21.5 %all-to-all-start.7 = ((bf16[32,16,128]{2,1,0:T(8,128)(2,1)}), bf16[32,16,128]{2,1,0:T(8,128)(2,1)S(1)}, u32[]{:S(2)}, u32[]{:S(2)}) async-start(bf16[32,16,128]{2,1,0:T(8,128)(2,1)} %broadcast_in_dim.21), calls=%async_computation.7 | async-start | bytes 262144 | tf_op jit(solution)/shard_map/all_to_all | solution.py:25
  357.7 10.9 %copy-start.4 = (f32[512,512]{1,0:T(8,128)S(1)}, f32[512,512]{1,0:T(8,128)}, u32[]{:S(2)}) copy-start(f32[512,512]{1,0:T(8,128)} %fusion.20) | copy-start | bytes 3145732
  369.9 7.8 %copy-start.6 = (bf16[16,32,8,128]{3,2,0,1:T(8,128)(2,1)S(1)}, bf16[16,32,8,128]{3,2,0,1:T(8,128)(2,1)}, u32[]{:S(2)}) copy-start(bf16[16,32,8,128]{3,2,0,1:T(8,128)(2,1)} %copy.60) | copy-start | bytes 3145732

commit v2 on v1

v2 whole, which is shorter than its diff:
```python
import math

import jax
import jax.numpy as jnp
from jax import lax
from jax.experimental import pallas as pl
from jax.experimental.pallas import tpu as pltpu
from jax.sharding import PartitionSpec as P

HEAD_DIM = 128
LANDMARKS = 512
ITERS = 3
ACROSS = ("z", "core")
PLANE = ("core", "space")
SCALE = 1.0 / math.sqrt(HEAD_DIM)
F32 = jnp.float32
BF16 = jnp.bfloat16


def softmax_rows(logits):
    ceiling = jnp.max(logits, axis=-1, keepdims=True)
    expo = jnp.exp(logits - ceiling)
    return expo / jnp.sum(expo, axis=-1, keepdims=True)


def halves(x):
    high = x.astype(BF16)
    return high, (x - high.astype(F32)).astype(BF16)


def triple(left, right):
    lh, ll = left
    rh, rl = right
    out = jnp.dot(lh, rh, preferred_element_type=F32)
    out += jnp.dot(lh, rl, preferred_element_type=F32)
    return out + jnp.dot(ll, rh, preferred_element_type=F32)


def inverse_body(q_ref, k_ref, out_ref, kh_ref, kl_ref):
    dims = (((1,), (1,)), ((), ()))
    q, k = q_ref[...], k_ref[...]
    logits = lax.dot_general(q, k, dims, preferred_element_type=F32) * SCALE
    kernel = softmax_rows(logits)
    column_top = jnp.max(jnp.sum(kernel, axis=0, keepdims=True))
    kh_ref[...], kl_ref[...] = halves(kernel)
    logits = lax.dot_general(k, q, dims, preferred_element_type=F32) * SCALE
    expo = jnp.exp(logits - jnp.max(logits, axis=0, keepdims=True))
    out_ref[...] = expo / (jnp.sum(expo, axis=0, keepdims=True) * column_top)

    def step(_, carry):
        iterate = out_ref[...]
        z = halves(iterate)
        y = halves(triple((kh_ref[...], kl_ref[...]), z))
        first = triple(z, y)
        second = triple(halves(first), y)
        third = triple(halves(second), y)
        out_ref[...] = 0.25 * (13.0 * iterate - 15.0 * first + 7.0 * second - third)
        return carry

    lax.fori_loop(0, ITERS, step, 0)


def pseudo_inverse(q_land, k_land):
    whole = pl.BlockSpec(memory_space=pltpu.VMEM)
    return pl.pallas_call(
        inverse_body,
        out_shape=jax.ShapeDtypeStruct((LANDMARKS, LANDMARKS), F32),
        in_specs=[whole, whole],
        out_specs=whole,
        scratch_shapes=[pltpu.VMEM((LANDMARKS, LANDMARKS), BF16)] * 2,
        compiler_params=pltpu.CompilerParams(vmem_limit_bytes=32 * 2**20),
        cost_estimate=pl.CostEstimate(
            flops=12 * 3 * 2 * LANDMARKS**3, bytes_accessed=2 * 2**20, transcendentals=0
        ),
    )(q_land, k_land)


def pack_body(q_ref, k_ref, v_ref, id_ref, out_ref):
    sides, part = id_ref.shape
    quad = out_ref.shape[0] // sides
    row = lax.broadcasted_iota(jnp.int32, (16, part), 0)
    for side in range(sides):
        ids = id_ref[side : side + 1, :]
        coarse = lax.shift_right_logical(ids, 8)
        fine = ids - coarse * 256
        tile = jnp.where(row == 0, coarse, jnp.where(row == 1, fine, 0))
        tile = tile.astype(F32).astype(BF16)
        rows = slice(side * part, (side + 1) * part)
        for head in range(quad):
            lanes = slice(head * HEAD_DIM, (head + 1) * HEAD_DIM)
            chunk = head * sides + side
            out_ref[chunk, :part, :] = q_ref[rows, lanes]
            out_ref[chunk, part : 2 * part, :] = k_ref[rows, lanes]
            out_ref[chunk, 2 * part : 3 * part, :] = v_ref[rows, lanes]
            out_ref[chunk, 3 * part : 3 * part + 16, :] = tile


def pack(queries, keys, values, groups, sides):
    count, width = queries.shape
    part = count // sides
    quad = 4
    columns = quad * HEAD_DIM
    cut = pl.BlockSpec((count, columns), lambda i: (0, i))
    rows = 3 * part + 16
    chunks = width // HEAD_DIM * sides
    return pl.pallas_call(
        pack_body,
        grid=(width // columns,),
        out_shape=jax.ShapeDtypeStruct((chunks, rows, HEAD_DIM), BF16),
        in_specs=[cut, cut, cut, pl.BlockSpec((sides, part), lambda i: (0, 0))],
        out_specs=pl.BlockSpec((quad * sides, rows, HEAD_DIM), lambda i: (i, 0, 0)),
        compiler_params=pltpu.CompilerParams(vmem_limit_bytes=24 * 2**20),
    )(queries, keys, values, groups.reshape(sides, part))


def unpack_body(in_ref, out_ref):
    chunks, part, _ = in_ref.shape
    sides = out_ref.shape[0] // part
    for chunk in range(chunks):
        head, side = chunk // sides, chunk % sides
        rows = slice(side * part, (side + 1) * part)
        out_ref[rows, head * HEAD_DIM : (head + 1) * HEAD_DIM] = in_ref[chunk]


def unpack(x, sides):
    chunks, part, _ = x.shape
    quad = 4
    return pl.pallas_call(
        unpack_body,
        grid=(chunks // sides // quad,),
        out_shape=jax.ShapeDtypeStruct((sides * part, chunks // sides * HEAD_DIM), BF16),
        in_specs=[pl.BlockSpec((quad * sides, part, HEAD_DIM), lambda i: (i, 0, 0))],
        out_specs=pl.BlockSpec((sides * part, quad * HEAD_DIM), lambda i: (0, i)),
        compiler_params=pltpu.CompilerParams(vmem_limit_bytes=24 * 2**20),
    )(x)


def swap(x, axes):
    return lax.all_to_all(x, axes, split_axis=0, concat_axis=0, tiled=True)


def share(x, axes):
    size = lax.axis_size(axes)
    return swap(jnp.broadcast_to(x[None], (size,) + x.shape), axes)


def local(queries, keys, values, groups):
    frames, count, width = queries.shape
    heads = width // HEAD_DIM
    sides = lax.axis_size("core")
    steps = heads * sides
    part = count // sides
    tokens = steps * part
    plane = lax.axis_size(PLANE)
    block = LANDMARKS // plane

    packed = pack(queries[0], keys[0], values[0], groups, sides)
    got = swap(packed, ACROSS)
    q = got[:, :part].reshape(tokens, HEAD_DIM)
    k = got[:, part : 2 * part].reshape(tokens, HEAD_DIM)
    v = got[:, 2 * part : 3 * part].reshape(tokens, HEAD_DIM)
    ids = got[:, 3 * part : 3 * part + 2].astype(F32)
    member = (ids[:, 0] * 256.0 + ids[:, 1]).astype(jnp.int32).reshape(tokens)

    landmark_ids = jnp.arange(LANDMARKS, dtype=jnp.int32)
    onehot = (member[None, :] == landmark_ids[:, None]).astype(BF16)
    q_part = jnp.dot(onehot, q, preferred_element_type=F32).astype(BF16)
    k_part = jnp.dot(onehot, k, preferred_element_type=F32).astype(BF16)
    members_each = plane * tokens // LANDMARKS
    both = jnp.concatenate(
        [q_part.reshape(plane, block, HEAD_DIM), k_part.reshape(plane, block, HEAD_DIM)], axis=1
    )
    sums = jnp.sum(swap(both, PLANE).astype(F32), axis=0)
    lands = share((sums / members_each).astype(BF16), PLANE)
    q_land = lands[:, :block].reshape(LANDMARKS, HEAD_DIM)
    k_land = lands[:, block:].reshape(LANDMARKS, HEAD_DIM)

    few = 8

    def split(x):
        x = x.reshape(steps, part // few, few, HEAD_DIM)
        return jnp.swapaxes(x, 0, 1).reshape(part // few, steps * few, HEAD_DIM)

    logits = jnp.einsum("sae,sbe->sab", split(q), split(k), preferred_element_type=F32) * SCALE
    index = jnp.arange(steps * few, dtype=jnp.int32) % few
    logits = jnp.where(index[:, None] == index[None, :], logits, -jnp.inf)
    weights = softmax_rows(logits).astype(BF16)
    temporal = jnp.einsum("sab,sbe->sae", weights, split(v), preferred_element_type=F32)
    temporal = temporal.astype(BF16).reshape(part // few, steps, few, HEAD_DIM)
    temporal = jnp.swapaxes(temporal, 0, 1).reshape(tokens, HEAD_DIM)

    land_logits = jnp.einsum("me,se->ms", q_land, k, preferred_element_type=F32) * SCALE
    own_top = jnp.max(land_logits, axis=-1, keepdims=True).astype(BF16)
    own_weights = jnp.exp(land_logits - own_top.astype(F32))
    own_total = jnp.sum(own_weights, axis=-1, keepdims=True)
    own_sum = jnp.dot(own_weights.astype(BF16), temporal, preferred_element_type=F32)
    high, low = halves(own_total)
    extra = jnp.pad(
        jnp.concatenate([own_top, high, low], axis=1), ((0, 0), (0, HEAD_DIM - 3))
    )
    own = jnp.concatenate([own_sum.astype(BF16), extra], axis=1)
    parts = swap(own.reshape(plane, block, 2 * HEAD_DIM), PLANE).astype(F32)
    tops = parts[:, :, HEAD_DIM : HEAD_DIM + 1]
    totals = parts[:, :, HEAD_DIM + 1 : HEAD_DIM + 2] + parts[:, :, HEAD_DIM + 2 : HEAD_DIM + 3]
    factor = jnp.exp(tops - jnp.max(tops, axis=0))
    weighted = jnp.sum(parts[:, :, :HEAD_DIM] * factor, axis=0)
    summary = (weighted / jnp.sum(totals * factor, axis=0)).astype(BF16)
    summary = share(summary, PLANE).reshape(LANDMARKS, HEAD_DIM).astype(F32)

    inverse = pseudo_inverse(q_land, k_land)
    token_logits = jnp.einsum("se,me->sm", q, k_land, preferred_element_type=F32) * SCALE
    attend = lax.optimization_barrier(softmax_rows(token_logits).astype(BF16))
    mixed = jnp.dot(inverse, summary, precision=lax.Precision.HIGHEST).astype(BF16)
    global_part = jnp.dot(attend, mixed, preferred_element_type=F32)
    combined = (temporal.astype(F32) + global_part).astype(BF16)
    back = swap(combined.reshape(steps, part, HEAD_DIM), ACROSS)
    return unpack(back, sides)[None]


def solution(mesh):
    tm, space = mesh.devices.shape
    fine = jax.sharding.Mesh(mesh.devices.reshape(tm // 2, 2, space), ("z", "core", "space"))
    block = P(("z", "core"), "space", None)
    return jax.shard_map(
        local,
        mesh=fine,
        in_specs=(block, block, block, P(("z", "core"), "space")),
        out_specs=block,
        check_vma=False,
    )
```

time: 457 us -> 314 us (0.69); the launches traced: 448 us -> 313 us
  blocking collectives: 115 us -> 63.2 us
  matrix products: 49.9 us -> 15.1 us
  starting transfers between devices: 65.4 us -> 37.6 us
  waiting for transfers between devices: 175 us -> 160 us
    dot_general x19 -> x9, matrix products: 49.9 us -> 15.1 us  [the longest x1 3.5 us: local(): global_part = jnp.dot(attend, mixed, preferred_element_type=F32)]
    all_to_all x2 -> x1, blocking collectives: 94.4 us -> 63.2 us  [swap(): return lax.all_to_all(x, axes, split_axis=0, concat_axis=0, tiled=True)]
    all_to_all x7 -> x5, starting transfers between devices: 65.4 us -> 37.6 us  [swap(): return lax.all_to_all(x, axes, split_axis=0, concat_axis=0, tiled=True)]
    all_gather x1 -> x0, blocking collectives: 20.3 us -> none  [local(): member = lax.all_gather(member, 'space')]
    unnamed x3 -> x0, Pallas kernels: 17.2 us -> none
    pallas_call x0 -> x3, Pallas kernels: none -> 16.1 us  [the longest x1 12 us: pseudo_inverse(): pl.pallas_call(inverse_body, out_shape=jax.ShapeDtypeStruct((LANDMARKS, L...]
    all_to_all x7 -> x5, waiting for transfers between devices: 175 us -> 160 us  [swap(): return lax.all_to_all(x, axes, split_axis=0, concat_axis=0, tiled=True)]
  transfers between devices with their start and end apart: 7 -> 5, of which waited for: 6 -> 4; matrix products, arithmetic and copies ran while one was open for 12% -> 4% of each run, Pallas kernels for 2% -> 4%
where the time goes in v2:
time: 314 us; the launch traced here: 313 us
  waiting for transfers between devices  160 us (51%)
  blocking collectives  63.2 us (20%)
  starting transfers between devices  37.6 us (12%)
  Pallas kernels  16.1 us (5%)
  matrix products  15.1 us (5%)
  local copies, waits for them, and re-layouts  10.7 us (3%)
  other arithmetic  10.7 us (3%)
    all_to_all x5, waiting for transfers between devices, swap(): return lax.all_to_all(x, axes, split_axis=0, concat_axis=0, tiled=True)  160 us
    all_to_all x1, blocking collectives, swap(): return lax.all_to_all(x, axes, split_axis=0, concat_axis=0, tiled=True)  63.2 us
    all_to_all x5, starting transfers between devices, swap(): return lax.all_to_all(x, axes, split_axis=0, concat_axis=0, tiled=True)  37.6 us
    pallas_call x1, Pallas kernels, pseudo_inverse(): pl.pallas_call(inverse_body, out_shape=jax.ShapeDtypeStruct((LANDMARKS, L...  12 us
  transfers between devices with their start and end apart: 5, of which 4 were waited for; matrix products, arithmetic and copies ran while one was open for 4% of the time, Pallas kernels for 4%

profile of v2, /device:TPU:1, one launch (start us, length us, event | category | flops | bytes accessed | tf_op | source)
XLA Modules:
  0.0 313.4 jit_solution(10111274332197688215)
XLA Ops:
  0.0 1.2 copy-done
  1.2 1.2 copy-done.1
  2.5 1.2 copy-done.2
  4.4 2.5 shard_map.46
  6.9 16.7 %all-to-all-start = ((bf16[32,400,128]{2,1,0:T(8,128)(2,1)}), bf16[32,400,128]{2,1,0:T(8,128)(2,1)S(1)}, u32[]{:S(2)}, u32[]{:S(2)}) async-start(bf16[32,400,128]{2,1,0:T(8,128)(2,1)} %shard_map.46), calls=%async_computation | async-start | bytes 6553600 | tf_op jit(solution)/shard_map/all_to_all | solution.py:139
  23.8 146.1 %all-to-all-done = bf16[32,400,128]{2,1,0:T(8,128)(2,1)S(1)} async-done(((bf16[32,400,128]{2,1,0:T(8,128)(2,1)}), bf16[32,400,128]{2,1,0:T(8,128)(2,1)S(1)}, u32[]{:S(2)}, u32[]{:S(2)}) %all-to-all-start) | async-done | bytes 3276832 | tf_op jit(solution)/shard_map/all_to_all | solution.py:139
  169.9 2.6 slice_bitcast_fusion
  172.5 1.4 fusion.19
  173.9 1.4 fusion.18
  175.3 0.7 pad_maximum_fusion
  176.0 8.0 %all-to-all-start.1 = ((bf16[32,32,128]{2,1,0:T(8,128)(2,1)}), bf16[32,32,128]{2,1,0:T(8,128)(2,1)S(1)}, u32[]{:S(2)}, u32[]{:S(2)}) async-start(bf16[32,32,128]{2,1,0:T(8,128)(2,1)} %pad_maximum_fusion), calls=%async_computation.1 | async-start | bytes 524288 | tf_op jit(solution)/shard_map/all_to_all | solution.py:139
  184.7 3.1 fusion.44
  187.8 5.0 %all-to-all-done.1 = bf16[32,32,128]{2,1,0:T(8,128)(2,1)S(1)} async-done(((bf16[32,32,128]{2,1,0:T(8,128)(2,1)}), bf16[32,32,128]{2,1,0:T(8,128)(2,1)S(1)}, u32[]{:S(2)}, u32[]{:S(2)}) %all-to-all-start.1) | async-done | bytes 262176 | tf_op jit(solution)/shard_map/all_to_all | solution.py:139
  192.9 0.7 broadcast_in_dim.16
  193.6 4.3 %all-to-all-start.2 = ((bf16[32,32,128]{2,1,0:T(8,128)(2,1)}), bf16[32,32,128]{2,1,0:T(8,128)(2,1)S(1)}, u32[]{:S(2)}, u32[]{:S(2)}) async-start(bf16[32,32,128]{2,1,0:T(8,128)(2,1)} %broadcast_in_dim.16), calls=%async_computation.2 | async-start | bytes 524288 | tf_op jit(solution)/shard_map/all_to_all | solution.py:139
  197.9 3.1 fusion.17
  201.3 5.4 %all-to-all-done.2 = bf16[32,32,128]{2,1,0:T(8,128)(2,1)S(1)} async-done(((bf16[32,32,128]{2,1,0:T(8,128)(2,1)}), bf16[32,32,128]{2,1,0:T(8,128)(2,1)S(1)}, u32[]{:S(2)}, u32[]{:S(2)}) %all-to-all-start.2) | async-done | bytes 262176 | tf_op jit(solution)/shard_map/all_to_all | solution.py:139
  206.8 1.3 multiply_reduce_fusion
  208.1 1.5 fusion.4
  209.7 1.8 fusion.20
  211.6 0.8 copy.36
  212.4 4.3 %all-to-all-start.3 = ((bf16[32,16,256]{2,1,0:T(8,128)(2,1)}), bf16[32,16,256]{2,1,0:T(8,128)(2,1)S(1)}, u32[]{:S(2)}, u32[]{:S(2)}) async-start(bf16[32,16,256]{2,1,0:T(8,128)(2,1)} %bitcast.24), calls=%async_computation.3 | async-start | bytes 524288 | tf_op jit(solution)/shard_map/all_to_all | solution.py:139
  216.7 1.3 multiply_reduce_fusion.1
  218.0 1.4 fusion.3
  219.4 3.0 divide_convert_fusion
  222.4 3.2 %all-to-all-done.3 = bf16[32,16,256]{2,1,0:T(8,128)(2,1)S(1)} async-done(((bf16[32,16,256]{2,1,0:T(8,128)(2,1)}), bf16[32,16,256]{2,1,0:T(8,128)(2,1)S(1)}, u32[]{:S(2)}, u32[]{:S(2)}) %all-to-all-start.3) | async-done | bytes 262176 | tf_op jit(solution)/shard_map/all_to_all | solution.py:139
  225.6 1.0 copy.37
  228.2 4.3 %all-to-all-start.4 = ((bf16[32,16,128]{2,1,0:T(8,128)(2,1)}), bf16[32,16,128]{2,1,0:T(8,128)(2,1)S(1)}, u32[]{:S(2)}, u32[]{:S(2)}) async-start(bf16[32,16,128]{2,1,0:T(8,128)(2,1)} %broadcast_in_dim.17), calls=%async_computation.4 | async-start | bytes 262144 | tf_op jit(solution)/shard_map/all_to_all | solution.py:139
  232.5 12.0 %shard_map.47 = f32[512,512]{1,0:T(8,128)S(1)} custom-call(bf16[512,128]{1,0:T(8,128)(2,1)S(1)} %bitcast.59, bf16[512,128]{1,0:T(8,128)(2,1)S(1)} %bitcast.61), custom_call_target="tpu_custom_call" | custom-call | flops 9663676416 | bytes 2097152 | tf_op jit(solution)/shard_map/pallas_call | solution.py:65
  245.2 3.5 %fusion.6 = bf16[4096,128]{1,0:T(8,128)(2,1)S(1)} fusion(bf16[4096,512]{0,1:T(8,128)(2,1)} %divide_convert_fusion, bf16[512,128]{1,0:T(8,128)(2,1)S(1)} %convolution_convert_fusion, bf16[4096,128]{1,0:T(8,128)(2,1)S(1)} %bitcast.64), kind=kOutput, calls=%fused_computation.13 | convolution fusion | flops 538443776 | bytes 6422528 | tf_op jit(solution)/shard_map/dot_general | solution.py:214
  248.7 63.2 %all_to_all.30.in_ref = bf16[32,128,128]{2,1,0:T(8,128)(2,1)S(1)} all-to-all(bf16[32,128,128]{2,1,0:T(8,128)(2,1)S(1)} %bitcast.65), channel_id=1, replica_groups=mesh['z'=16,'core'=2,'space'=16] {'z','core'}, dimensions={0} | all-to-all | bytes 2097152 | tf_op jit(solution)/shard_map/all_to_all | solution.py:139
  311.8 1.6 shard_map.48
  (43 shorter events, 4.2 us)
Async XLA Ops:
  0.0 1.2 copy-start
  1.2 1.2 copy-start.1
  2.5 1.2 copy-start.2
  3.7 0.7 copy-start.3
  6.9 163.0 %all-to-all-start = ((bf16[32,400,128]{2,1,0:T(8,128)(2,1)}), bf16[32,400,128]{2,1,0:T(8,128)(2,1)S(1)}, u32[]{:S(2)}, u32[]{:S(2)}) async-start(bf16[32,400,128]{2,1,0:T(8,128)(2,1)} %shard_map.46), calls=%async_computation | async-start | bytes 6553600 | tf_op jit(solution)/shard_map/all_to_all | solution.py:139
  172.5 2.8 copy-start.4
  172.5 2.8 copy-start.8
  172.5 11.5 %copy-start.6 = (bf16[16,32,8,128]{3,2,0,1:T(8,128)(2,1)S(1)}, bf16[16,32,8,128]{3,2,0,1:T(8,128)(2,1)}, u32[]{:S(2)}) copy-start(bf16[16,32,8,128]{3,2,0,1:T(8,128)(2,1)} %get-tuple-element.6) | copy-start | bytes 3145732
  172.5 11.5 %copy-start.7 = (bf16[16,32,8,128]{3,2,0,1:T(8,128)(2,1)S(1)}, bf16[16,32,8,128]{3,2,0,1:T(8,128)(2,1)}, u32[]{:S(2)}) copy-start(bf16[16,32,8,128]{3,2,0,1:T(8,128)(2,1)} %get-tuple-element.7) | copy-start | bytes 3145732
  176.0 16.8 %all-to-all-start.1 = ((bf16[32,32,128]{2,1,0:T(8,128)(2,1)}), bf16[32,32,128]{2,1,0:T(8,128)(2,1)S(1)}, u32[]{:S(2)}, u32[]{:S(2)}) async-start(bf16[32,32,128]{2,1,0:T(8,128)(2,1)} %pad_maximum_fusion), calls=%async_computation.1 | async-start | bytes 524288 | tf_op jit(solution)/shard_map/all_to_all | solution.py:139
  184.7 13.2 %copy-start.10 = (bf16[16,32,8,128]{3,2,0,1:T(8,128)(2,1)S(1)}, bf16[16,32,8,128]{3,2,0,1:T(8,128)(2,1)}, u32[]{:S(2)}) copy-start(bf16[16,32,8,128]{3,2,0,1:T(8,128)(2,1)} %get-tuple-element.5) | copy-start | bytes 3145732
  193.6 13.1 %all-to-all-start.2 = ((bf16[32,32,128]{2,1,0:T(8,128)(2,1)}), bf16[32,32,128]{2,1,0:T(8,128)(2,1)S(1)}, u32[]{:S(2)}, u32[]{:S(2)}) async-start(bf16[32,32,128]{2,1,0:T(8,128)(2,1)} %broadcast_in_dim.16), calls=%async_computation.2 | async-start | bytes 524288 | tf_op jit(solution)/shard_map/all_to_all | solution.py:139
  197.9 8.8 %copy-start.9 = (bf16[32,128,128]{2,1,0:T(8,128)(2,1)S(1)}, bf16[32,128,128]{2,1,0:T(8,128)(2,1)}, u32[]{:S(2)}) copy-start(bf16[32,128,128]{2,1,0:T(8,128)(2,1)} %copy-done.8) | copy-start | bytes 3145732
  209.7 7.1 %copy-start.5 = (bf16[32,128,128]{2,1,0:T(8,128)(2,1)S(1)}, bf16[32,128,128]{2,1,0:T(8,128)(2,1)}, u32[]{:S(2)}) copy-start(bf16[32,128,128]{2,1,0:T(8,128)(2,1)} %copy-done.4) | copy-start | bytes 3145732
  212.4 13.1 %all-to-all-start.3 = ((bf16[32,16,256]{2,1,0:T(8,128)(2,1)}), bf16[32,16,256]{2,1,0:T(8,128)(2,1)S(1)}, u32[]{:S(2)}, u32[]{:S(2)}) async-start(bf16[32,16,256]{2,1,0:T(8,128)(2,1)} %bitcast.24), calls=%async_computation.3 | async-start | bytes 524288 | tf_op jit(solution)/shard_map/all_to_all | solution.py:139
  228.2 16.3 %all-to-all-start.4 = ((bf16[32,16,128]{2,1,0:T(8,128)(2,1)}), bf16[32,16,128]{2,1,0:T(8,128)(2,1)S(1)}, u32[]{:S(2)}, u32[]{:S(2)}) async-start(bf16[32,16,128]{2,1,0:T(8,128)(2,1)} %broadcast_in_dim.17), calls=%async_computation.4 | async-start | bytes 262144 | tf_op jit(solution)/shard_map/all_to_all | solution.py:139

commit v3 on v2

--- a/solution.py
+++ b/solution.py
@@ -36,7 +36,7 @@
     return out + jnp.dot(ll, rh, preferred_element_type=F32)
 
 
-def inverse_body(q_ref, k_ref, out_ref, kh_ref, kl_ref):
+def inverse_body(q_ref, k_ref, high_ref, low_ref, out_ref, kh_ref, kl_ref):
     dims = (((1,), (1,)), ((), ()))
     q, k = q_ref[...], k_ref[...]
     logits = lax.dot_general(q, k, dims, preferred_element_type=F32) * SCALE
@@ -58,16 +58,18 @@
         return carry
 
     lax.fori_loop(0, ITERS, step, 0)
+    high_ref[...], low_ref[...] = halves(out_ref[...])
 
 
 def pseudo_inverse(q_land, k_land):
     whole = pl.BlockSpec(memory_space=pltpu.VMEM)
     return pl.pallas_call(
         inverse_body,
-        out_shape=jax.ShapeDtypeStruct((LANDMARKS, LANDMARKS), F32),
+        out_shape=[jax.ShapeDtypeStruct((LANDMARKS, LANDMARKS), BF16)] * 2,
         in_specs=[whole, whole],
-        out_specs=whole,
-        scratch_shapes=[pltpu.VMEM((LANDMARKS, LANDMARKS), BF16)] * 2,
+        out_specs=[whole, whole],
+        scratch_shapes=[pltpu.VMEM((LANDMARKS, LANDMARKS), F32)]
+        + [pltpu.VMEM((LANDMARKS, LANDMARKS), BF16)] * 2,
         compiler_params=pltpu.CompilerParams(vmem_limit_bytes=32 * 2**20),
         cost_estimate=pl.CostEstimate(
             flops=12 * 3 * 2 * LANDMARKS**3, bytes_accessed=2 * 2**20, transcendentals=0
@@ -109,7 +111,7 @@
         out_shape=jax.ShapeDtypeStruct((chunks, rows, HEAD_DIM), BF16),
         in_specs=[cut, cut, cut, pl.BlockSpec((sides, part), lambda i: (0, 0))],
         out_specs=pl.BlockSpec((quad * sides, rows, HEAD_DIM), lambda i: (i, 0, 0)),
-        compiler_params=pltpu.CompilerParams(vmem_limit_bytes=24 * 2**20),
+        compiler_params=pltpu.CompilerParams(vmem_limit_bytes=56 * 2**20),
     )(queries, keys, values, groups.reshape(sides, part))
 
 
@@ -135,6 +137,145 @@
     )(x)
 
 
+def local_call(body, out_shape, operands, megabytes, scratch=(), flops=0):
+    whole = pl.BlockSpec(memory_space=pltpu.VMEM)
+    size = sum(x.size * x.dtype.itemsize for x in operands)
+    return pl.pallas_call(
+        body,
+        out_shape=out_shape,
+        in_specs=[whole] * len(operands),
+        out_specs=whole,
+        scratch_shapes=list(scratch),
+        compiler_params=pltpu.CompilerParams(vmem_limit_bytes=megabytes * 2**20),
+        cost_estimate=pl.CostEstimate(flops=flops, bytes_accessed=size, transcendentals=0),
+    )(*operands)
+
+
+def sums_body(got_ref, out_ref, acc_ref):
+    steps = got_ref.shape[0]
+    part = (got_ref.shape[1] - 16) // 3
+    plane, pair, _ = out_ref.shape
+    block = pair // 2
+    several = 4
+    rows = lax.broadcasted_iota(jnp.int32, (LANDMARKS, part), 0)
+    acc_ref[...] = jnp.zeros_like(acc_ref)
+
+    def step(turn, carry):
+        onehot, rest = [], []
+        for inner in range(several):
+            frame = turn * several + inner
+            ids = got_ref[frame, 3 * part : 3 * part + 16, :].astype(F32)
+            member = (ids[0:1, :] * 256.0 + ids[1:2, :]).astype(jnp.int32)
+            onehot.append((rows == member).astype(F32).astype(BF16))
+            rest.append(
+                jnp.concatenate(
+                    [got_ref[frame, :part, :], got_ref[frame, part : 2 * part, :]], axis=1
+                )
+            )
+        acc_ref[...] += jnp.dot(
+            jnp.concatenate(onehot, axis=1),
+            jnp.concatenate(rest, axis=0),
+            preferred_element_type=F32,
+        )
+        return carry
+
+    lax.fori_loop(0, steps // several, step, 0)
+    for side in range(2):
+        x = acc_ref[:, side * HEAD_DIM : (side + 1) * HEAD_DIM].astype(BF16)
+        out_ref[:, side * block : (side + 1) * block, :] = x.reshape(plane, block, HEAD_DIM)
+
+
+def group_sums(got, plane):
+    pair = 2 * LANDMARKS // plane
+    return local_call(
+        sums_body,
+        jax.ShapeDtypeStruct((plane, pair, HEAD_DIM), BF16),
+        [got],
+        24,
+        [pltpu.VMEM((LANDMARKS, 2 * HEAD_DIM), F32)],
+        flops=4 * LANDMARKS * 4096 * HEAD_DIM,
+    )
+
+
+def combine_body(parts_ref, out_ref):
+    x = parts_ref[...].astype(F32)
+    tops = x[:, :, HEAD_DIM : HEAD_DIM + 1]
+    totals = x[:, :, HEAD_DIM + 1 : HEAD_DIM + 2] + x[:, :, HEAD_DIM + 2 : HEAD_DIM + 3]
+    factor = jnp.exp(tops - jnp.max(tops, axis=0, keepdims=True))
+    weighted = jnp.sum(x[:, :, :HEAD_DIM] * factor, axis=0, keepdims=True)
+    total = jnp.sum(totals * factor, axis=0, keepdims=True)
+    out_ref[...] = jnp.broadcast_to((weighted / total).astype(BF16), out_ref.shape)
+
+
+def combine(parts):
+    plane, block, _ = parts.shape
+    return local_call(
+        combine_body, jax.ShapeDtypeStruct((plane, block, HEAD_DIM), BF16), [parts], 16
+    )
+
+
+def attend_body(got_ref, land_ref, out_ref):
+    steps = got_ref.shape[0]
+    part = (got_ref.shape[1] - 16) // 3
+    several = 4
+    land = land_ref[...]
+
+    def step(turn, carry):
+        tile = got_ref[pl.ds(turn * several, several), :part, :].reshape(several * part, HEAD_DIM)
+        logits = lax.dot_general(
+            tile, land, (((1,), (1,)), ((), ())), preferred_element_type=F32
+        )
+        logits = logits * SCALE
+        expo = jnp.exp(logits - jnp.max(logits, axis=1, keepdims=True))
+        weights = expo / jnp.sum(expo, axis=1, keepdims=True)
+        start = pl.multiple_of(turn * several * part, several * part)
+        out_ref[pl.ds(start, several * part), :] = weights.astype(BF16)
+        return carry
+
+    lax.fori_loop(0, steps // several, step, 0)
+
+
+def token_weights(got, k_land):
+    steps, rows, _ = got.shape
+    tokens = steps * ((rows - 16) // 3)
+    return local_call(
+        attend_body,
+        jax.ShapeDtypeStruct((tokens, LANDMARKS), BF16),
+        [got, k_land],
+        24,
+        flops=2 * LANDMARKS * tokens * HEAD_DIM * 4,
+    )
+
+
+def final_body(high_ref, low_ref, summary_ref, attend_ref, temporal_ref, out_ref):
+    steps, part, _ = out_ref.shape
+    several = 4
+    summary = summary_ref[...].reshape(LANDMARKS, HEAD_DIM)
+    mixed = jnp.dot(high_ref[...], summary, preferred_element_type=F32)
+    mixed += jnp.dot(low_ref[...], summary, preferred_element_type=F32)
+    mixed = mixed.astype(BF16)
+
+    def step(turn, carry):
+        start = pl.multiple_of(turn * several * part, several * part)
+        rows = pl.ds(start, several * part)
+        tile = jnp.dot(attend_ref[rows, :], mixed, preferred_element_type=F32)
+        tile = (tile + temporal_ref[rows, :].astype(F32)).astype(BF16)
+        out_ref[pl.ds(turn * several, several)] = tile.reshape(several, part, HEAD_DIM)
+        return carry
+
+    lax.fori_loop(0, steps // several, step, 0)
+
+
+def finish(high, low, summary, attend, temporal, steps, part):
+    return local_call(
+        final_body,
+        jax.ShapeDtypeStruct((steps, part, HEAD_DIM), BF16),
+        [high, low, summary, attend, temporal],
+        24,
+        flops=4 * LANDMARKS * steps * part * HEAD_DIM,
+    )
+
+
 def swap(x, axes):
     return lax.all_to_all(x, axes, split_axis=0, concat_axis=0, tiled=True)
 
@@ -159,18 +300,8 @@
     q = got[:, :part].reshape(tokens, HEAD_DIM)
     k = got[:, part : 2 * part].reshape(tokens, HEAD_DIM)
     v = got[:, 2 * part : 3 * part].reshape(tokens, HEAD_DIM)
-    ids = got[:, 3 * part : 3 * part + 2].astype(F32)
-    member = (ids[:, 0] * 256.0 + ids[:, 1]).astype(jnp.int32).reshape(tokens)
-
-    landmark_ids = jnp.arange(LANDMARKS, dtype=jnp.int32)
-    onehot = (member[None, :] == landmark_ids[:, None]).astype(BF16)
-    q_part = jnp.dot(onehot, q, preferred_element_type=F32).astype(BF16)
-    k_part = jnp.dot(onehot, k, preferred_element_type=F32).astype(BF16)
     members_each = plane * tokens // LANDMARKS
-    both = jnp.concatenate(
-        [q_part.reshape(plane, block, HEAD_DIM), k_part.reshape(plane, block, HEAD_DIM)], axis=1
-    )
-    sums = jnp.sum(swap(both, PLANE).astype(F32), axis=0)
+    sums = jnp.sum(swap(group_sums(got, plane), PLANE).astype(F32), axis=0)
     lands = share((sums / members_each).astype(BF16), PLANE)
     q_land = lands[:, :block].reshape(LANDMARKS, HEAD_DIM)
     k_land = lands[:, block:].reshape(LANDMARKS, HEAD_DIM)
@@ -199,21 +330,13 @@
         jnp.concatenate([own_top, high, low], axis=1), ((0, 0), (0, HEAD_DIM - 3))
     )
     own = jnp.concatenate([own_sum.astype(BF16), extra], axis=1)
-    parts = swap(own.reshape(plane, block, 2 * HEAD_DIM), PLANE).astype(F32)
-    tops = parts[:, :, HEAD_DIM : HEAD_DIM + 1]
-    totals = parts[:, :, HEAD_DIM + 1 : HEAD_DIM + 2] + parts[:, :, HEAD_DIM + 2 : HEAD_DIM + 3]
-    factor = jnp.exp(tops - jnp.max(tops, axis=0))
-    weighted = jnp.sum(parts[:, :, :HEAD_DIM] * factor, axis=0)
-    summary = (weighted / jnp.sum(totals * factor, axis=0)).astype(BF16)
-    summary = share(summary, PLANE).reshape(LANDMARKS, HEAD_DIM).astype(F32)
-
-    inverse = pseudo_inverse(q_land, k_land)
-    token_logits = jnp.einsum("se,me->sm", q, k_land, preferred_element_type=F32) * SCALE
-    attend = lax.optimization_barrier(softmax_rows(token_logits).astype(BF16))
-    mixed = jnp.dot(inverse, summary, precision=lax.Precision.HIGHEST).astype(BF16)
-    global_part = jnp.dot(attend, mixed, preferred_element_type=F32)
-    combined = (temporal.astype(F32) + global_part).astype(BF16)
-    back = swap(combined.reshape(steps, part, HEAD_DIM), ACROSS)
+    high, low = pseudo_inverse(q_land, k_land)
+    parts = swap(own.reshape(plane, block, 2 * HEAD_DIM), PLANE)
+    parts, high, low = lax.optimization_barrier((parts, high, low))
+    summary = swap(combine(parts), PLANE)
+    attend = token_weights(got, k_land)
+    out = finish(high, low, summary, attend, temporal, steps, part)
+    back = swap(out, ACROSS)
     return unpack(back, sides)[None]
 
 

time: 314 us -> 319 us (1.016)
  Pallas kernels: 16.1 us -> 28.9 us
  local copies, waits for them, and re-layouts: 10.7 us -> 18.2 us
  waiting for transfers between devices: 160 us -> 153 us
  matrix products: 15.1 us -> 8.44 us
  other arithmetic: 10.7 us -> 5.42 us
  starting transfers between devices: 37.6 us -> 40.9 us
    pallas_call x1 -> x5, Pallas kernels: 12 us -> 22.9 us  [the longest x1 12.2 us: pseudo_inverse(): pl.pallas_call(inverse_body, out_shape=[jax.ShapeDtypeStruct((LANDMARKS,...]
    dot_general x5 -> x0, matrix products: 8.15 us -> none  [the longest x1 3.5 us: local(): global_part = jnp.dot(attend, mixed, preferred_element_type=F32)]
    unnamed x22 -> x28, local copies, waits for them, and re-layouts: 4.38 us -> 12.5 us
    all_to_all x5, waiting for transfers between devices: 160 us -> 153 us  [swap(): return lax.all_to_all(x, axes, split_axis=0, concat_axis=0, tiled=True)]
    all_to_all x5, starting transfers between devices: 37.6 us -> 40.9 us  [swap(): return lax.all_to_all(x, axes, split_axis=0, concat_axis=0, tiled=True)]
  transfers between devices with their start and end apart: 5 -> 5, of which waited for: 4 -> 4; matrix products, arithmetic and copies ran while one was open for 4% -> 4% of each run, Pallas kernels for 4% -> 5%
where the time goes in v3:
time: 319 us; the launch traced here: 318 us
  waiting for transfers between devices  153 us (48%)
  blocking collectives  63.3 us (20%)
  starting transfers between devices  40.9 us (13%)
  Pallas kernels  28.9 us (9%)
  local copies, waits for them, and re-layouts  18.2 us (6%)
  matrix products  8.44 us (3%)
  other arithmetic  5.42 us (2%)
    all_to_all x5, waiting for transfers between devices, swap(): return lax.all_to_all(x, axes, split_axis=0, concat_axis=0, tiled=True)  153 us
    all_to_all x1, blocking collectives, swap(): return lax.all_to_all(x, axes, split_axis=0, concat_axis=0, tiled=True)  63.3 us
    all_to_all x5, starting transfers between devices, swap(): return lax.all_to_all(x, axes, split_axis=0, concat_axis=0, tiled=True)  40.9 us
    unnamed x28, local copies, waits for them, and re-layouts  12.5 us
    pallas_call x1, Pallas kernels, pseudo_inverse(): pl.pallas_call(inverse_body, out_shape=[jax.ShapeDtypeStruct((LANDMARKS,...  12.2 us
    pallas_call x4, Pallas kernels, local_call(): pl.pallas_call(body, out_shape=out_shape, in_specs=[whole] * len(operands...  10.7 us
  transfers between devices with their start and end apart: 5, of which 4 were waited for; matrix products, arithmetic and copies ran while one was open for 4% of the time, Pallas kernels for 5%

profile of v3, /device:TPU:1, one launch (start us, length us, event | category | flops | bytes accessed | tf_op | source)
XLA Modules:
  0.0 318.2 jit_solution(13133872129564233493)
XLA Ops:
  0.0 4.4 %shard_map.46 = bf16[32,400,128]{2,1,0:T(8,128)(2,1)} custom-call(bf16[256,2048]{1,0:T(8,128)(2,1)} %bitcast.47, bf16[256,2048]{1,0:T(8,128)(2,1)} %bitcast.48, bf16[256,2048]{1,0:T(8,128)(2,1)} %bitcast.49, s32[2,128]{1,0:T(2,128)} %bitcast.52), custom_call_target="tpu_custom_call" | custom-call | tf_op jit(solution)/shard_map/pallas_call | solution.py:108
  4.4 16.7 %all-to-all-start = ((bf16[32,400,128]{2,1,0:T(8,128)(2,1)}), bf16[32,400,128]{2,1,0:T(8,128)(2,1)S(1)}, u32[]{:S(2)}, u32[]{:S(2)}) async-start(bf16[32,400,128]{2,1,0:T(8,128)(2,1)} %shard_map.46), calls=%async_computation | async-start | bytes 6553600 | tf_op jit(solution)/shard_map/all_to_all | solution.py:280
  21.9 145.5 %all-to-all-done.got_ref = bf16[32,400,128]{2,1,0:T(8,128)(2,1)S(1)} async-done(((bf16[32,400,128]{2,1,0:T(8,128)(2,1)}), bf16[32,400,128]{2,1,0:T(8,128)(2,1)S(1)}, u32[]{:S(2)}, u32[]{:S(2)}) %all-to-all-start) | async-done | bytes 3276832 | tf_op jit(solution)/shard_map/all_to_all | solution.py:280
  167.3 3.2 %shard_map.47 = bf16[32,32,128]{2,1,0:T(8,128)(2,1)} custom-call(bf16[32,400,128]{2,1,0:T(8,128)(2,1)S(1)} %all-to-all-done.got_ref), custom_call_target="tpu_custom_call" | custom-call | flops 1073741824 | bytes 3276800 | tf_op jit(solution)/shard_map/pallas_call | solution.py:143
  170.6 8.0 %all-to-all-start.1 = ((bf16[32,32,128]{2,1,0:T(8,128)(2,1)}), bf16[32,32,128]{2,1,0:T(8,128)(2,1)S(1)}, u32[]{:S(2)}, u32[]{:S(2)}) async-start(bf16[32,32,128]{2,1,0:T(8,128)(2,1)} %shard_map.47), calls=%async_computation.1 | async-start | bytes 524288 | tf_op jit(solution)/shard_map/all_to_all | solution.py:280
  178.6 2.1 slice_bitcast_fusion
  181.5 3.1 fusion.31
  184.6 2.8 all-to-all-done.1
  188.2 4.6 %all-to-all-start.2 = ((bf16[32,32,128]{2,1,0:T(8,128)(2,1)}), bf16[32,32,128]{2,1,0:T(8,128)(2,1)S(1)}, u32[]{:S(2)}, u32[]{:S(2)}) async-start(bf16[32,32,128]{2,1,0:T(8,128)(2,1)} %broadcast_in_dim.12), calls=%async_computation.2 | async-start | bytes 524288 | tf_op jit(solution)/shard_map/all_to_all | solution.py:280
  192.8 3.3 %fusion.11 = bf16[16,32,8,128]{3,2,1,0:T(8,128)(2,1)S(1)} fusion(f32[16,256,256]{1,2,0:T(8,128)} %get-tuple-element.24, f32[16,256]{1,0:T(8,128)S(1)} %get-tuple-element.23, bf16[16,32,8,128]{3,2,0,1:T(8,128)(2,1)} %get-tuple-element.15), kind=kOutput, calls=%fused_computation.15 | convolution fusion | flops 271056896 | bytes 6307840 | tf_op jit(solution)/shard_map/sab,sbe->sae/dot_general | solution.py:319
  196.1 1.3 copy.9
  197.4 4.3 %all-to-all-done.2 = bf16[32,32,128]{2,1,0:T(8,128)(2,1)S(1)} async-done(((bf16[32,32,128]{2,1,0:T(8,128)(2,1)}), bf16[32,32,128]{2,1,0:T(8,128)(2,1)S(1)}, u32[]{:S(2)}, u32[]{:S(2)}) %all-to-all-start.2) | async-done | bytes 262176 | tf_op jit(solution)/shard_map/all_to_all | solution.py:280
  202.3 2.6 multiply_reduce_fusion
  204.9 1.5 fusion.1
  206.5 1.8 fusion.12
  208.4 0.8 copy.10
  209.2 4.3 %all-to-all-start.3 = ((bf16[32,16,256]{2,1,0:T(8,128)(2,1)}), bf16[32,16,256]{2,1,0:T(8,128)(2,1)S(1)}, u32[]{:S(2)}, u32[]{:S(2)}) async-start(bf16[32,16,256]{2,1,0:T(8,128)(2,1)} %bitcast.46), calls=%async_computation.3 | async-start | bytes 524288 | tf_op jit(solution)/shard_map/all_to_all | solution.py:280
  213.5 0.9 copy-done.5
  214.4 0.9 copy-done.11
  215.3 12.2 %shard_map.48 = (bf16[512,512]{1,0:T(8,128)(2,1)S(1)}, bf16[512,512]{1,0:T(8,128)(2,1)S(1)}) custom-call(bf16[512,128]{1,0:T(8,128)(2,1)S(1)} %bitcast.42, bf16[512,128]{1,0:T(8,128)(2,1)S(1)} %bitcast.43), custom_call_target="tpu_custom_call" | custom-call | flops 9663676416 | bytes 2097152 | tf_op jit(solution)/shard_map/pallas_call | solution.py:66
  228.3 0.8 copy-done.8
  230.1 7.3 %all-to-all-start.4 = ((bf16[32,16,128]{2,1,0:T(8,128)(2,1)}), bf16[32,16,128]{2,1,0:T(8,128)(2,1)S(1)}, u32[]{:S(2)}, u32[]{:S(2)}) async-start(bf16[32,16,128]{2,1,0:T(8,128)(2,1)} %copy-done.10), calls=%async_computation.4 | async-start | bytes 262144 | tf_op jit(solution)/shard_map/all_to_all | solution.py:280
  237.4 0.9 copy-done.12
  238.3 4.4 %shard_map.50.attend_ref = bf16[4096,512]{1,0:T(8,128)(2,1)S(1)} custom-call(bf16[32,400,128]{2,1,0:T(8,128)(2,1)S(1)} %all-to-all-done.got_ref, bf16[512,128]{1,0:T(8,128)(2,1)S(1)} %bitcast.44), custom_call_target="tpu_custom_call" | custom-call | flops 2147483648 | bytes 3407872 | tf_op jit(solution)/shard_map/pallas_call | solution.py:143
  242.7 1.9 copy-done.2
  245.0 1.2 copy-done.1
  246.2 2.2 copy-done.3
  248.4 1.0 copy-done.7
  249.4 1.0 copy-done.9
  250.5 2.8 shard_map.51
  253.3 63.3 %all_to_all.30.in_ref = bf16[32,128,128]{2,1,0:T(8,128)(2,1)S(1)} all-to-all(bf16[32,128,128]{2,1,0:T(8,128)(2,1)S(1)} %shard_map.51), channel_id=1, replica_groups=mesh['z'=16,'core'=2,'space'=16] {'z','core'}, dimensions={0} | all-to-all | bytes 2097152 | tf_op jit(solution)/shard_map/all_to_all | solution.py:280
  316.6 1.6 shard_map.52
  (35 shorter events, 5.2 us)
Async XLA Ops:
  4.4 163.0 %all-to-all-start = ((bf16[32,400,128]{2,1,0:T(8,128)(2,1)}), bf16[32,400,128]{2,1,0:T(8,128)(2,1)S(1)}, u32[]{:S(2)}, u32[]{:S(2)}) async-start(bf16[32,400,128]{2,1,0:T(8,128)(2,1)} %shard_map.46), calls=%async_computation | async-start | bytes 6553600 | tf_op jit(solution)/shard_map/all_to_all | solution.py:280
  170.6 16.8 %all-to-all-start.1 = ((bf16[32,32,128]{2,1,0:T(8,128)(2,1)}), bf16[32,32,128]{2,1,0:T(8,128)(2,1)S(1)}, u32[]{:S(2)}, u32[]{:S(2)}) async-start(bf16[32,32,128]{2,1,0:T(8,128)(2,1)} %shard_map.47), calls=%async_computation.1 | async-start | bytes 524288 | tf_op jit(solution)/shard_map/all_to_all | solution.py:280
  180.7 0.8 copy-start.13
  188.2 13.4 %all-to-all-start.2 = ((bf16[32,32,128]{2,1,0:T(8,128)(2,1)}), bf16[32,32,128]{2,1,0:T(8,128)(2,1)S(1)}, u32[]{:S(2)}, u32[]{:S(2)}) async-start(bf16[32,32,128]{2,1,0:T(8,128)(2,1)} %broadcast_in_dim.12), calls=%async_computation.2 | async-start | bytes 524288 | tf_op jit(solution)/shard_map/all_to_all | solution.py:280
  202.3 2.6 copy-start.4
  204.9 1.5 copy-start
  209.2 19.9 %all-to-all-start.3 = ((bf16[32,16,256]{2,1,0:T(8,128)(2,1)}), bf16[32,16,256]{2,1,0:T(8,128)(2,1)S(1)}, u32[]{:S(2)}, u32[]{:S(2)}) async-start(bf16[32,16,256]{2,1,0:T(8,128)(2,1)} %bitcast.46), calls=%async_computation.3 | async-start | bytes 524288 | tf_op jit(solution)/shard_map/all_to_all | solution.py:280
  213.5 0.9 copy-start.5
  214.4 0.9 copy-start.11
  227.5 0.8 copy-start.6
  228.3 0.8 copy-start.8
  229.4 0.7 copy-start.10
  230.1 14.9 %all-to-all-start.4 = ((bf16[32,16,128]{2,1,0:T(8,128)(2,1)}), bf16[32,16,128]{2,1,0:T(8,128)(2,1)S(1)}, u32[]{:S(2)}, u32[]{:S(2)}) async-start(bf16[32,16,128]{2,1,0:T(8,128)(2,1)} %copy-done.10), calls=%async_computation.4 | async-start | bytes 262144 | tf_op jit(solution)/shard_map/all_to_all | solution.py:280
  237.4 0.9 copy-start.12
  242.7 1.9 copy-start.2
  245.0 1.2 copy-start.1
  246.2 2.2 copy-start.3
  248.4 1.0 copy-start.7
  249.4 1.0 copy-start.9

commit v4 on v2

--- a/solution.py
+++ b/solution.py
@@ -10,6 +10,7 @@
 HEAD_DIM = 128
 LANDMARKS = 512
 ITERS = 3
+GROUP = 256
 ACROSS = ("z", "core")
 PLANE = ("core", "space")
 SCALE = 1.0 / math.sqrt(HEAD_DIM)
@@ -31,12 +32,21 @@
 def triple(left, right):
     lh, ll = left
     rh, rl = right
-    out = jnp.dot(lh, rh, preferred_element_type=F32)
-    out += jnp.dot(lh, rl, preferred_element_type=F32)
-    return out + jnp.dot(ll, rh, preferred_element_type=F32)
-
-
-def inverse_body(q_ref, k_ref, out_ref, kh_ref, kl_ref):
+    return jnp.dot(
+        jnp.concatenate([lh, lh, ll], axis=1),
+        jnp.concatenate([rh, rl, rh], axis=0),
+        preferred_element_type=F32,
+    )
+
+
+def newton(iterate, z, y):
+    first = triple(z, y)
+    second = triple(halves(first), y)
+    third = triple(halves(second), y)
+    return 0.25 * (13.0 * iterate - 15.0 * first + 7.0 * second - third)
+
+
+def inverse_body(q_ref, k_ref, zh_ref, zl_ref, yh_ref, yl_ref, out_ref, kh_ref, kl_ref):
     dims = (((1,), (1,)), ((), ()))
     q, k = q_ref[...], k_ref[...]
     logits = lax.dot_general(q, k, dims, preferred_element_type=F32) * SCALE
@@ -51,28 +61,52 @@
         iterate = out_ref[...]
         z = halves(iterate)
         y = halves(triple((kh_ref[...], kl_ref[...]), z))
-        first = triple(z, y)
-        second = triple(halves(first), y)
-        third = triple(halves(second), y)
-        out_ref[...] = 0.25 * (13.0 * iterate - 15.0 * first + 7.0 * second - third)
+        out_ref[...] = newton(iterate, z, y)
         return carry
 
-    lax.fori_loop(0, ITERS, step, 0)
-
-
-def pseudo_inverse(q_land, k_land):
-    whole = pl.BlockSpec(memory_space=pltpu.VMEM)
-    return pl.pallas_call(
+    lax.fori_loop(0, ITERS - 1, step, 0)
+    z = halves(out_ref[...])
+    zh_ref[...], zl_ref[...] = z
+    yh_ref[...], yl_ref[...] = halves(triple((kh_ref[...], kl_ref[...]), z))
+
+
+def whole_call(body, out_shape, operands, megabytes, scratch=(), flops=0):
+    size = sum(x.size * x.dtype.itemsize for x in operands)
+    return pl.pallas_call(
+        body,
+        out_shape=out_shape,
+        scratch_shapes=list(scratch),
+        compiler_params=pltpu.CompilerParams(vmem_limit_bytes=megabytes * 2**20),
+        cost_estimate=pl.CostEstimate(flops=flops, bytes_accessed=size, transcendentals=0),
+    )(*operands)
+
+
+def inverse_parts(q_land, k_land):
+    return whole_call(
         inverse_body,
-        out_shape=jax.ShapeDtypeStruct((LANDMARKS, LANDMARKS), F32),
-        in_specs=[whole, whole],
-        out_specs=whole,
-        scratch_shapes=[pltpu.VMEM((LANDMARKS, LANDMARKS), BF16)] * 2,
-        compiler_params=pltpu.CompilerParams(vmem_limit_bytes=32 * 2**20),
-        cost_estimate=pl.CostEstimate(
-            flops=12 * 3 * 2 * LANDMARKS**3, bytes_accessed=2 * 2**20, transcendentals=0
-        ),
-    )(q_land, k_land)
+        [jax.ShapeDtypeStruct((LANDMARKS, LANDMARKS), BF16)] * 4,
+        [q_land, k_land],
+        24,
+        [pltpu.VMEM((LANDMARKS, LANDMARKS), F32)] + [pltpu.VMEM((LANDMARKS, LANDMARKS), BF16)] * 2,
+        flops=9 * 3 * 2 * LANDMARKS**3,
+    )
+
+
+def last_body(zh_ref, zl_ref, yh_ref, yl_ref, high_ref, low_ref):
+    z = (zh_ref[...], zl_ref[...])
+    y = (yh_ref[...], yl_ref[...])
+    iterate = z[0].astype(F32) + z[1].astype(F32)
+    high_ref[...], low_ref[...] = halves(newton(iterate, z, y))
+
+
+def last_iteration(parts):
+    return whole_call(
+        last_body,
+        [jax.ShapeDtypeStruct((LANDMARKS, LANDMARKS), BF16)] * 2,
+        list(parts),
+        24,
+        flops=3 * 3 * 2 * LANDMARKS**3,
+    )
 
 
 def pack_body(q_ref, k_ref, v_ref, id_ref, out_ref):
@@ -109,7 +143,7 @@
         out_shape=jax.ShapeDtypeStruct((chunks, rows, HEAD_DIM), BF16),
         in_specs=[cut, cut, cut, pl.BlockSpec((sides, part), lambda i: (0, 0))],
         out_specs=pl.BlockSpec((quad * sides, rows, HEAD_DIM), lambda i: (i, 0, 0)),
-        compiler_params=pltpu.CompilerParams(vmem_limit_bytes=24 * 2**20),
+        compiler_params=pltpu.CompilerParams(vmem_limit_bytes=12 * 2**20),
     )(queries, keys, values, groups.reshape(sides, part))
 
 
@@ -131,17 +165,152 @@
         out_shape=jax.ShapeDtypeStruct((sides * part, chunks // sides * HEAD_DIM), BF16),
         in_specs=[pl.BlockSpec((quad * sides, part, HEAD_DIM), lambda i: (i, 0, 0))],
         out_specs=pl.BlockSpec((sides * part, quad * HEAD_DIM), lambda i: (0, i)),
-        compiler_params=pltpu.CompilerParams(vmem_limit_bytes=24 * 2**20),
+        compiler_params=pltpu.CompilerParams(vmem_limit_bytes=12 * 2**20),
     )(x)
+
+
+def sums_body(got_ref, out_ref, acc_ref):
+    several = got_ref.shape[0]
+    part = (got_ref.shape[1] - 16) // 3
+    plane, pair, _ = out_ref.shape
+    block = pair // 2
+    turn = pl.program_id(0)
+
+    @pl.when(turn == 0)
+    def _():
+        acc_ref[...] = jnp.zeros_like(acc_ref)
+
+    rows = lax.broadcasted_iota(jnp.int32, (LANDMARKS, part), 0)
+    onehot, rest = [], []
+    for frame in range(several):
+        ids = got_ref[frame, 3 * part : 3 * part + 16, :].astype(F32)
+        member = (ids[0:1, :] * 256.0 + ids[1:2, :]).astype(jnp.int32)
+        onehot.append((rows == member).astype(F32).astype(BF16))
+        rest.append(
+            jnp.concatenate([got_ref[frame, :part, :], got_ref[frame, part : 2 * part, :]], axis=1)
+        )
+    acc_ref[...] += jnp.dot(
+        jnp.concatenate(onehot, axis=1),
+        jnp.concatenate(rest, axis=0),
+        preferred_element_type=F32,
+    )
+
+    @pl.when(turn == pl.num_programs(0) - 1)
+    def _():
+        for side in range(2):
+            x = acc_ref[:, side * HEAD_DIM : (side + 1) * HEAD_DIM].astype(BF16)
+            out_ref[:, side * block : (side + 1) * block, :] = x.reshape(plane, block, HEAD_DIM)
+
+
+def group_sums(got, plane):
+    steps, rows, _ = got.shape
+    several = 4
+    pair = 2 * LANDMARKS // plane
+    return pl.pallas_call(
+        sums_body,
+        grid=(steps // several,),
+        out_shape=jax.ShapeDtypeStruct((plane, pair, HEAD_DIM), BF16),
+        in_specs=[pl.BlockSpec((several, rows, HEAD_DIM), lambda i: (i, 0, 0))],
+        out_specs=pl.BlockSpec((plane, pair, HEAD_DIM), lambda i: (0, 0, 0)),
+        scratch_shapes=[pltpu.VMEM((LANDMARKS, 2 * HEAD_DIM), F32)],
+        compiler_params=pltpu.CompilerParams(vmem_limit_bytes=12 * 2**20),
+    )(got)
+
+
+def mean_body(parts_ref, out_ref):
+    total = jnp.sum(parts_ref[...].astype(F32), axis=0, keepdims=True)
+    mean = (total / GROUP).astype(BF16)
+    out_ref[...] = jnp.broadcast_to(mean, out_ref.shape)
+
+
+def group_means(parts):
+    return whole_call(mean_body, jax.ShapeDtypeStruct(parts.shape, BF16), [parts], 8)
+
+
+def combine_body(parts_ref, out_ref):
+    x = parts_ref[...].astype(F32)
+    tops = x[:, :, HEAD_DIM : HEAD_DIM + 1]
+    totals = x[:, :, HEAD_DIM + 1 : HEAD_DIM + 2] + x[:, :, HEAD_DIM + 2 : HEAD_DIM + 3]
+    factor = jnp.exp(tops - jnp.max(tops, axis=0, keepdims=True))
+    weighted = jnp.sum(x[:, :, :HEAD_DIM] * factor, axis=0, keepdims=True)
+    total = jnp.sum(totals * factor, axis=0, keepdims=True)
+    out_ref[...] = jnp.broadcast_to((weighted / total).astype(BF16), out_ref.shape)
+
+
+def combine(parts):
+    plane, block, _ = parts.shape
+    return whole_call(
+        combine_body, jax.ShapeDtypeStruct((plane, block, HEAD_DIM), BF16), [parts], 8
+    )
+
+
+def attend_body(tile_ref, land_ref, out_ref):
+    tile = tile_ref[...].reshape(out_ref.shape[0], HEAD_DIM)
+    logits = lax.dot_general(
+        tile, land_ref[...], (((1,), (1,)), ((), ())), preferred_element_type=F32
+    )
+    logits = logits * SCALE
+    expo = jnp.exp(logits - jnp.max(logits, axis=1, keepdims=True))
+    out_ref[...] = (expo / jnp.sum(expo, axis=1, keepdims=True)).astype(BF16)
+
+
+def token_weights(got, k_land):
+    steps, rows, _ = got.shape
+    part = (rows - 16) // 3
+    several = 4
+    return pl.pallas_call(
+        attend_body,
+        grid=(steps // several,),
+        out_shape=jax.ShapeDtypeStruct((steps * part, LANDMARKS), BF16),
+        in_specs=[
+            pl.BlockSpec((several, part, HEAD_DIM), lambda i: (i, 0, 0)),
+            pl.BlockSpec((LANDMARKS, HEAD_DIM), lambda i: (0, 0)),
+        ],
+        out_specs=pl.BlockSpec((several * part, LANDMARKS), lambda i: (i, 0)),
+        compiler_params=pltpu.CompilerParams(vmem_limit_bytes=12 * 2**20),
+        cost_estimate=pl.CostEstimate(
+            flops=8 * LANDMARKS * steps * part * HEAD_DIM,
+            bytes_accessed=5 * 2**20,
+            transcendentals=0,
+        ),
+    )(got, k_land)
+
+
+def final_body(high_ref, low_ref, summary_ref, attend_ref, temporal_ref, out_ref, mixed_ref):
+    @pl.when(pl.program_id(0) == 0)
+    def _():
+        summary = summary_ref[...].reshape(LANDMARKS, HEAD_DIM)
+        mixed = jnp.dot(high_ref[...], summary, preferred_element_type=F32)
+        mixed += jnp.dot(low_ref[...], summary, preferred_element_type=F32)
+        mixed_ref[...] = mixed.astype(BF16)
+
+    tile = jnp.dot(attend_ref[...], mixed_ref[...], preferred_element_type=F32)
+    tile = (tile + temporal_ref[...].astype(F32)).astype(BF16)
+    out_ref[...] = tile.reshape(out_ref.shape)
+
+
+def finish(high, low, summary, attend, temporal, steps, part):
+    several = 8
+    square = pl.BlockSpec((LANDMARKS, LANDMARKS), lambda i: (0, 0))
+    return pl.pallas_call(
+        final_body,
+        grid=(steps // several,),
+        out_shape=jax.ShapeDtypeStruct((steps, part, HEAD_DIM), BF16),
+        in_specs=[
+            square,
+            square,
+            pl.BlockSpec(summary.shape, lambda i: (0, 0, 0)),
+            pl.BlockSpec((several * part, LANDMARKS), lambda i: (i, 0)),
+            pl.BlockSpec((several * part, HEAD_DIM), lambda i: (i, 0)),
+        ],
+        out_specs=pl.BlockSpec((several, part, HEAD_DIM), lambda i: (i, 0, 0)),
+        scratch_shapes=[pltpu.VMEM((LANDMARKS, HEAD_DIM), BF16)],
+        compiler_params=pltpu.CompilerParams(vmem_limit_bytes=16 * 2**20),
+    )(high, low, summary, attend, temporal)
 
 
 def swap(x, axes):
     return lax.all_to_all(x, axes, split_axis=0, concat_axis=0, tiled=True)
-
-
-def share(x, axes):
-    size = lax.axis_size(axes)
-    return swap(jnp.broadcast_to(x[None], (size,) + x.shape), axes)
 
 
 def local(queries, keys, values, groups):
@@ -159,19 +328,7 @@
     q = got[:, :part].reshape(tokens, HEAD_DIM)
     k = got[:, part : 2 * part].reshape(tokens, HEAD_DIM)
     v = got[:, 2 * part : 3 * part].reshape(tokens, HEAD_DIM)
-    ids = got[:, 3 * part : 3 * part + 2].astype(F32)
-    member = (ids[:, 0] * 256.0 + ids[:, 1]).astype(jnp.int32).reshape(tokens)
-
-    landmark_ids = jnp.arange(LANDMARKS, dtype=jnp.int32)
-    onehot = (member[None, :] == landmark_ids[:, None]).astype(BF16)
-    q_part = jnp.dot(onehot, q, preferred_element_type=F32).astype(BF16)
-    k_part = jnp.dot(onehot, k, preferred_element_type=F32).astype(BF16)
-    members_each = plane * tokens // LANDMARKS
-    both = jnp.concatenate(
-        [q_part.reshape(plane, block, HEAD_DIM), k_part.reshape(plane, block, HEAD_DIM)], axis=1
-    )
-    sums = jnp.sum(swap(both, PLANE).astype(F32), axis=0)
-    lands = share((sums / members_each).astype(BF16), PLANE)
+    lands = swap(group_means(swap(group_sums(got, plane), PLANE)), PLANE)
     q_land = lands[:, :block].reshape(LANDMARKS, HEAD_DIM)
     k_land = lands[:, block:].reshape(LANDMARKS, HEAD_DIM)
 
@@ -199,21 +356,14 @@
         jnp.concatenate([own_top, high, low], axis=1), ((0, 0), (0, HEAD_DIM - 3))
     )
     own = jnp.concatenate([own_sum.astype(BF16), extra], axis=1)
-    parts = swap(own.reshape(plane, block, 2 * HEAD_DIM), PLANE).astype(F32)
-    tops = parts[:, :, HEAD_DIM : HEAD_DIM + 1]
-    totals = parts[:, :, HEAD_DIM + 1 : HEAD_DIM + 2] + parts[:, :, HEAD_DIM + 2 : HEAD_DIM + 3]
-    factor = jnp.exp(tops - jnp.max(tops, axis=0))
-    weighted = jnp.sum(parts[:, :, :HEAD_DIM] * factor, axis=0)
-    summary = (weighted / jnp.sum(totals * factor, axis=0)).astype(BF16)
-    summary = share(summary, PLANE).reshape(LANDMARKS, HEAD_DIM).astype(F32)
-
-    inverse = pseudo_inverse(q_land, k_land)
-    token_logits = jnp.einsum("se,me->sm", q, k_land, preferred_element_type=F32) * SCALE
-    attend = lax.optimization_barrier(softmax_rows(token_logits).astype(BF16))
-    mixed = jnp.dot(inverse, summary, precision=lax.Precision.HIGHEST).astype(BF16)
-    global_part = jnp.dot(attend, mixed, preferred_element_type=F32)
-    combined = (temporal.astype(F32) + global_part).astype(BF16)
-    back = swap(combined.reshape(steps, part, HEAD_DIM), ACROSS)
+    inverse = inverse_parts(q_land, k_land)
+    parts = swap(own.reshape(plane, block, 2 * HEAD_DIM), PLANE)
+    parts, inverse = lax.optimization_barrier((parts, inverse))
+    summary = swap(combine(parts), PLANE)
+    attend = token_weights(got, k_land)
+    high, low = last_iteration(inverse)
+    out = finish(high, low, summary, attend, temporal, steps, part)
+    back = swap(out, ACROSS)
     return unpack(back, sides)[None]
 
 

time: 314 us -> 323 us (1.029)
  local copies, waits for them, and re-layouts: 10.7 us -> 25.1 us
  Pallas kernels: 16.1 us -> 25.4 us
  waiting for transfers between devices: 160 us -> 153 us
  matrix products: 15.1 us -> 8.45 us
  other arithmetic: 10.7 us -> 5.35 us
  starting transfers between devices: 37.6 us -> 40.9 us
    unnamed x22 -> x44, local copies, waits for them, and re-layouts: 4.38 us -> 20.1 us
    pallas_call x1 -> x7, Pallas kernels: 12 us -> 22.9 us  [the longest x4 13 us: whole_call(): pl.pallas_call(body, out_shape=out_shape, scratch_shapes=list(scratch), c...]
    dot_general x5 -> x0, matrix products: 8.15 us -> none  [the longest x1 3.5 us: local(): global_part = jnp.dot(attend, mixed, preferred_element_type=F32)]
    all_to_all x5, waiting for transfers between devices: 160 us -> 153 us  [swap(): return lax.all_to_all(x, axes, split_axis=0, concat_axis=0, tiled=True)]
    all_to_all x5, starting transfers between devices: 37.6 us -> 40.9 us  [swap(): return lax.all_to_all(x, axes, split_axis=0, concat_axis=0, tiled=True)]
  transfers between devices with their start and end apart: 5 -> 5, of which waited for: 4 -> 4; matrix products, arithmetic and copies ran while one was open for 4% -> 3% of each run, Pallas kernels for 4% -> 5%
where the time goes in v4:
time: 323 us; the launch traced here: 322 us
  waiting for transfers between devices  153 us (47%)
  blocking collectives  63.3 us (20%)
  starting transfers between devices  40.9 us (13%)
  Pallas kernels  25.4 us (8%)
  local copies, waits for them, and re-layouts  25.1 us (8%)
  matrix products  8.45 us (3%)
  other arithmetic  5.35 us (2%)
    all_to_all x5, waiting for transfers between devices, swap(): return lax.all_to_all(x, axes, split_axis=0, concat_axis=0, tiled=True)  153 us
    all_to_all x1, blocking collectives, swap(): return lax.all_to_all(x, axes, split_axis=0, concat_axis=0, tiled=True)  63.3 us
    all_to_all x5, starting transfers between devices, swap(): return lax.all_to_all(x, axes, split_axis=0, concat_axis=0, tiled=True)  40.9 us
    unnamed x44, local copies, waits for them, and re-layouts  20.1 us
    pallas_call x4, Pallas kernels, whole_call(): pl.pallas_call(body, out_shape=out_shape, scratch_shapes=list(scratch), c...  13 us
  transfers between devices with their start and end apart: 5, of which 4 were waited for; matrix products, arithmetic and copies ran while one was open for 3% of the time, Pallas kernels for 5%

profile of v4, /device:TPU:1, one launch (start us, length us, event | category | flops | bytes accessed | tf_op | source)
XLA Modules:
  0.0 321.9 jit_solution(7809906370823569611)
XLA Ops:
  0.0 1.2 copy-done.6
  1.2 1.2 copy-done.7
  2.5 1.2 copy-done.8
  5.2 1.7 copy-done
  6.9 16.7 %all-to-all-start = ((bf16[32,400,128]{2,1,0:T(8,128)(2,1)}), bf16[32,400,128]{2,1,0:T(8,128)(2,1)S(1)}, u32[]{:S(2)}, u32[]{:S(2)}) async-start(bf16[32,400,128]{2,1,0:T(8,128)(2,1)} %copy-done), calls=%async_computation | async-start | bytes 6553600 | tf_op jit(solution)/shard_map/all_to_all | solution.py:313
  24.4 145.5 %all-to-all-done.got_ref.tile_ref = bf16[32,400,128]{2,1,0:T(8,128)(2,1)S(1)} async-done(((bf16[32,400,128]{2,1,0:T(8,128)(2,1)}), bf16[32,400,128]{2,1,0:T(8,128)(2,1)S(1)}, u32[]{:S(2)}, u32[]{:S(2)}) %all-to-all-start) | async-done | bytes 3276832 | tf_op jit(solution)/shard_map/all_to_all | solution.py:313
  169.9 3.2 %shard_map.47 = bf16[32,32,128]{2,1,0:T(8,128)(2,1)} custom-call(bf16[32,400,128]{2,1,0:T(8,128)(2,1)S(1)} %all-to-all-done.got_ref.tile_ref), custom_call_target="tpu_custom_call" | custom-call | tf_op jit(solution)/shard_map/pallas_call | solution.py:209
  173.1 8.0 %all-to-all-start.1 = ((bf16[32,32,128]{2,1,0:T(8,128)(2,1)}), bf16[32,32,128]{2,1,0:T(8,128)(2,1)S(1)}, u32[]{:S(2)}, u32[]{:S(2)}) async-start(bf16[32,32,128]{2,1,0:T(8,128)(2,1)} %shard_map.47), calls=%async_computation.1 | async-start | bytes 524288 | tf_op jit(solution)/shard_map/all_to_all | solution.py:313
  181.1 2.2 slice_bitcast_fusion
  184.1 3.1 fusion.31
  187.1 2.8 all-to-all-done.1.parts_ref
  190.7 4.6 %all-to-all-start.2 = ((bf16[32,32,128]{2,1,0:T(8,128)(2,1)}), bf16[32,32,128]{2,1,0:T(8,128)(2,1)S(1)}, u32[]{:S(2)}, u32[]{:S(2)}) async-start(bf16[32,32,128]{2,1,0:T(8,128)(2,1)} %copy-done.5), calls=%async_computation.2 | async-start | bytes 524288 | tf_op jit(solution)/shard_map/all_to_all | solution.py:313
  195.3 3.3 %fusion.11 = bf16[16,32,8,128]{3,2,1,0:T(8,128)(2,1)S(1)} fusion(f32[16,256,256]{1,2,0:T(8,128)} %get-tuple-element.36, f32[16,256]{1,0:T(8,128)S(1)} %get-tuple-element.35, bf16[16,32,8,128]{3,2,0,1:T(8,128)(2,1)} %get-tuple-element.27), kind=kOutput, calls=%fused_computation.15 | convolution fusion | flops 271056896 | bytes 6307840 | tf_op jit(solution)/shard_map/sab,sbe->sae/dot_general | solution.py:345
  198.6 1.3 copy.9
  199.9 4.3 %all-to-all-done.2 = bf16[32,32,128]{2,1,0:T(8,128)(2,1)S(1)} async-done(((bf16[32,32,128]{2,1,0:T(8,128)(2,1)}), bf16[32,32,128]{2,1,0:T(8,128)(2,1)S(1)}, u32[]{:S(2)}, u32[]{:S(2)}) %all-to-all-start.2) | async-done | bytes 262176 | tf_op jit(solution)/shard_map/all_to_all | solution.py:313
  204.8 2.6 multiply_reduce_fusion
  207.4 1.5 fusion.1
  209.0 1.8 fusion.12
  211.7 4.3 %all-to-all-start.3 = ((bf16[32,16,256]{2,1,0:T(8,128)(2,1)}), bf16[32,16,256]{2,1,0:T(8,128)(2,1)S(1)}, u32[]{:S(2)}, u32[]{:S(2)}) async-start(bf16[32,16,256]{2,1,0:T(8,128)(2,1)} %bitcast.50), calls=%async_computation.3 | async-start | bytes 524288 | tf_op jit(solution)/shard_map/all_to_all | solution.py:313
  217.8 9.2 %shard_map.49 = (bf16[512,512]{1,0:T(8,128)(2,1)S(1)}, bf16[512,512]{1,0:T(8,128)(2,1)S(1)}, bf16[512,512]{1,0:T(8,128)(2,1)S(1)}, bf16[512,512]{1,0:T(8,128)(2,1)S(1)}) custom-call(bf16[512,128]{1,0:T(8,128)(2,1)S(1)} %bitcast.45, bf16[512,128]{1,0:T(8,128)(2,1)S(1)} %bitcast.46), custom_call_target="tpu_custom_call" | custom-call | flops 7247757312 | bytes 262144 | tf_op jit(solution)/shard_map/pallas_call | solution.py:75
  230.3 4.5 %shard_map.52.attend_ref = bf16[4096,512]{1,0:T(8,128)(2,1)S(1)} custom-call(bf16[32,400,128]{2,1,0:T(8,128)(2,1)S(1)} %all-to-all-done.got_ref.tile_ref, bf16[512,128]{1,0:T(8,128)(2,1)S(1)} %bitcast.47), custom_call_target="tpu_custom_call" | custom-call | flops 2147483648 | bytes 5242880 | tf_op jit(solution)/shard_map/pallas_call | solution.py:261
  234.7 1.9 copy-done.3
  237.7 7.3 %all-to-all-start.4 = ((bf16[32,16,128]{2,1,0:T(8,128)(2,1)}), bf16[32,16,128]{2,1,0:T(8,128)(2,1)S(1)}, u32[]{:S(2)}, u32[]{:S(2)}) async-start(bf16[32,16,128]{2,1,0:T(8,128)(2,1)} %shard_map.51), calls=%async_computation.4 | async-start | bytes 262144 | tf_op jit(solution)/shard_map/all_to_all | solution.py:313
  245.0 1.0 copy-done.14
  246.1 1.0 copy-done.16
  247.1 1.0 copy-done.18
  248.1 1.0 copy-done.20
  249.2 2.7 shard_map.50
  252.5 2.2 copy-done.4
  254.7 2.2 shard_map.53
  257.0 63.3 %all_to_all.30.in_ref = bf16[32,128,128]{2,1,0:T(8,128)(2,1)S(1)} all-to-all(bf16[32,128,128]{2,1,0:T(8,128)(2,1)S(1)} %shard_map.53), channel_id=1, replica_groups=mesh['z'=16,'core'=2,'space'=16] {'z','core'}, dimensions={0} | all-to-all | bytes 2097152 | tf_op jit(solution)/shard_map/all_to_all | solution.py:313
  320.3 1.6 shard_map.54
  (50 shorter events, 12.1 us)
Async XLA Ops:
  0.0 1.2 copy-start.6
  1.2 1.2 copy-start.7
  2.5 1.2 copy-start.8
  3.7 0.7 copy-start.12
  5.2 1.7 copy-start
  6.9 163.0 %all-to-all-start = ((bf16[32,400,128]{2,1,0:T(8,128)(2,1)}), bf16[32,400,128]{2,1,0:T(8,128)(2,1)S(1)}, u32[]{:S(2)}, u32[]{:S(2)}) async-start(bf16[32,400,128]{2,1,0:T(8,128)(2,1)} %copy-done), calls=%async_computation | async-start | bytes 6553600 | tf_op jit(solution)/shard_map/all_to_all | solution.py:313
  173.1 16.8 %all-to-all-start.1 = ((bf16[32,32,128]{2,1,0:T(8,128)(2,1)}), bf16[32,32,128]{2,1,0:T(8,128)(2,1)S(1)}, u32[]{:S(2)}, u32[]{:S(2)}) async-start(bf16[32,32,128]{2,1,0:T(8,128)(2,1)} %shard_map.47), calls=%async_computation.1 | async-start | bytes 524288 | tf_op jit(solution)/shard_map/all_to_all | solution.py:313
  183.2 0.8 copy-start.21
  189.9 0.7 copy-start.5
  190.7 13.4 %all-to-all-start.2 = ((bf16[32,32,128]{2,1,0:T(8,128)(2,1)}), bf16[32,32,128]{2,1,0:T(8,128)(2,1)S(1)}, u32[]{:S(2)}, u32[]{:S(2)}) async-start(bf16[32,32,128]{2,1,0:T(8,128)(2,1)} %copy-done.5), calls=%async_computation.2 | async-start | bytes 524288 | tf_op jit(solution)/shard_map/all_to_all | solution.py:313
  204.8 2.6 copy-start.9
  207.4 1.5 copy-start.1
  211.7 24.9 %all-to-all-start.3 = ((bf16[32,16,256]{2,1,0:T(8,128)(2,1)}), bf16[32,16,256]{2,1,0:T(8,128)(2,1)S(1)}, u32[]{:S(2)}, u32[]{:S(2)}) async-start(bf16[32,16,256]{2,1,0:T(8,128)(2,1)} %bitcast.50), calls=%async_computation.3 | async-start | bytes 524288 | tf_op jit(solution)/shard_map/all_to_all | solution.py:313
  216.0 0.9 copy-start.10
  216.9 0.9 copy-start.11
  227.0 0.8 copy-start.13
  227.8 0.8 copy-start.15
  228.6 0.8 copy-start.17
  229.5 0.8 copy-start.19
  234.7 1.9 copy-start.3
  237.7 14.9 %all-to-all-start.4 = ((bf16[32,16,128]{2,1,0:T(8,128)(2,1)}), bf16[32,16,128]{2,1,0:T(8,128)(2,1)S(1)}, u32[]{:S(2)}, u32[]{:S(2)}) async-start(bf16[32,16,128]{2,1,0:T(8,128)(2,1)} %shard_map.51), calls=%async_computation.4 | async-start | bytes 262144 | tf_op jit(solution)/shard_map/all_to_all | solution.py:313
  245.0 1.0 copy-start.14
  246.1 1.0 copy-start.16
  247.1 1.0 copy-start.18
  248.1 1.0 copy-start.20
  249.2 3.4 %copy-start.2 = (bf16[16,32,8,128]{3,2,0,1:T(8,128)(2,1)S(1)}, bf16[16,32,8,128]{3,2,0,1:T(8,128)(2,1)}, u32[]{:S(2)}) copy-start(bf16[16,32,8,128]{3,2,0,1:T(8,128)(2,1)} %copy.9) | copy-start | bytes 3145732
  252.5 2.2 copy-start.4

commit v5 on v4

--- a/solution.py
+++ b/solution.py
@@ -22,6 +22,10 @@
     ceiling = jnp.max(logits, axis=-1, keepdims=True)
     expo = jnp.exp(logits - ceiling)
     return expo / jnp.sum(expo, axis=-1, keepdims=True)
+
+
+def in_hbm(*arrays):
+    return [pltpu.with_memory_space_constraint(x, pltpu.HBM) for x in arrays]
 
 
 def halves(x):
@@ -84,8 +88,8 @@
 def inverse_parts(q_land, k_land):
     return whole_call(
         inverse_body,
-        [jax.ShapeDtypeStruct((LANDMARKS, LANDMARKS), BF16)] * 4,
-        [q_land, k_land],
+        [pltpu.HBM((LANDMARKS, LANDMARKS), BF16)] * 4,
+        in_hbm(q_land, k_land),
         24,
         [pltpu.VMEM((LANDMARKS, LANDMARKS), F32)] + [pltpu.VMEM((LANDMARKS, LANDMARKS), BF16)] * 2,
         flops=9 * 3 * 2 * LANDMARKS**3,
@@ -102,8 +106,8 @@
 def last_iteration(parts):
     return whole_call(
         last_body,
-        [jax.ShapeDtypeStruct((LANDMARKS, LANDMARKS), BF16)] * 2,
-        list(parts),
+        [pltpu.HBM((LANDMARKS, LANDMARKS), BF16)] * 2,
+        in_hbm(*parts),
         24,
         flops=3 * 3 * 2 * LANDMARKS**3,
     )
@@ -140,11 +144,11 @@
     return pl.pallas_call(
         pack_body,
         grid=(width // columns,),
-        out_shape=jax.ShapeDtypeStruct((chunks, rows, HEAD_DIM), BF16),
+        out_shape=pltpu.HBM((chunks, rows, HEAD_DIM), BF16),
         in_specs=[cut, cut, cut, pl.BlockSpec((sides, part), lambda i: (0, 0))],
         out_specs=pl.BlockSpec((quad * sides, rows, HEAD_DIM), lambda i: (i, 0, 0)),
         compiler_params=pltpu.CompilerParams(vmem_limit_bytes=12 * 2**20),
-    )(queries, keys, values, groups.reshape(sides, part))
+    )(*in_hbm(queries, keys, values, groups.reshape(sides, part)))
 
 
 def unpack_body(in_ref, out_ref):
@@ -209,7 +213,7 @@
     return pl.pallas_call(
         sums_body,
         grid=(steps // several,),
-        out_shape=jax.ShapeDtypeStruct((plane, pair, HEAD_DIM), BF16),
+        out_shape=pltpu.HBM((plane, pair, HEAD_DIM), BF16),
         in_specs=[pl.BlockSpec((several, rows, HEAD_DIM), lambda i: (i, 0, 0))],
         out_specs=pl.BlockSpec((plane, pair, HEAD_DIM), lambda i: (0, 0, 0)),
         scratch_shapes=[pltpu.VMEM((LANDMARKS, 2 * HEAD_DIM), F32)],
@@ -224,7 +228,7 @@
 
 
 def group_means(parts):
-    return whole_call(mean_body, jax.ShapeDtypeStruct(parts.shape, BF16), [parts], 8)
+    return whole_call(mean_body, pltpu.HBM(parts.shape, BF16), [parts], 8)
 
 
 def combine_body(parts_ref, out_ref):
@@ -240,7 +244,7 @@
 def combine(parts):
     plane, block, _ = parts.shape
     return whole_call(
-        combine_body, jax.ShapeDtypeStruct((plane, block, HEAD_DIM), BF16), [parts], 8
+        combine_body, pltpu.HBM((plane, block, HEAD_DIM), BF16), [parts], 8
     )
 
 
@@ -261,7 +265,7 @@
     return pl.pallas_call(
         attend_body,
         grid=(steps // several,),
-        out_shape=jax.ShapeDtypeStruct((steps * part, LANDMARKS), BF16),
+        out_shape=pltpu.HBM((steps * part, LANDMARKS), BF16),
         in_specs=[
             pl.BlockSpec((several, part, HEAD_DIM), lambda i: (i, 0, 0)),
             pl.BlockSpec((LANDMARKS, HEAD_DIM), lambda i: (0, 0)),
@@ -273,7 +277,7 @@
             bytes_accessed=5 * 2**20,
             transcendentals=0,
         ),
-    )(got, k_land)
+    )(got, *in_hbm(k_land))
 
 
 def final_body(high_ref, low_ref, summary_ref, attend_ref, temporal_ref, out_ref, mixed_ref):
@@ -306,7 +310,7 @@
         out_specs=pl.BlockSpec((several, part, HEAD_DIM), lambda i: (i, 0, 0)),
         scratch_shapes=[pltpu.VMEM((LANDMARKS, HEAD_DIM), BF16)],
         compiler_params=pltpu.CompilerParams(vmem_limit_bytes=16 * 2**20),
-    )(high, low, summary, attend, temporal)
+    )(*in_hbm(high, low), summary, *in_hbm(attend, temporal))
 
 
 def swap(x, axes):
@@ -358,9 +362,9 @@
     own = jnp.concatenate([own_sum.astype(BF16), extra], axis=1)
     inverse = inverse_parts(q_land, k_land)
     parts = swap(own.reshape(plane, block, 2 * HEAD_DIM), PLANE)
-    parts, inverse = lax.optimization_barrier((parts, inverse))
+    parts, inverse, k_late = lax.optimization_barrier((parts, inverse, k_land))
     summary = swap(combine(parts), PLANE)
-    attend = token_weights(got, k_land)
+    attend = token_weights(got, k_late)
     high, low = last_iteration(inverse)
     out = finish(high, low, summary, attend, temporal, steps, part)
     back = swap(out, ACROSS)

time: 323 us -> 315 us (0.975)
  local copies, waits for them, and re-layouts: 25.1 us -> 5.04 us
  Pallas kernels: 25.4 us -> 39.3 us
    unnamed x44 -> x6, local copies, waits for them, and re-layouts: 20.1 us -> 0.14 us
    pallas_call x3, Pallas kernels: 8.57 us -> 14.5 us  [the longest x1 6.88 us: token_weights(): pl.pallas_call(attend_body, grid=(steps // several,), out_shape=pltpu.HBM...]
    pallas_call x4, Pallas kernels: 13 us -> 18.2 us  [whole_call(): pl.pallas_call(body, out_shape=out_shape, scratch_shapes=list(scratch), c...]
  transfers between devices with their start and end apart: 5 -> 5, of which waited for: 4 -> 3; matrix products, arithmetic and copies ran while one was open for 3% -> 4% of each run, Pallas kernels for 5% -> 7%
where the time goes in v5:
time: 315 us
  waiting for transfers between devices  153 us (49%)
  blocking collectives  62.9 us (20%)
  starting transfers between devices  40.9 us (13%)
  Pallas kernels  39.3 us (12%)
  matrix products  8.44 us (3%)
  other arithmetic  5.35 us (2%)
  local copies, waits for them, and re-layouts  5.04 us (2%)
    all_to_all x5, waiting for transfers between devices, swap(): return lax.all_to_all(x, axes, split_axis=0, concat_axis=0, tiled=True)  153 us
    all_to_all x1, blocking collectives, swap(): return lax.all_to_all(x, axes, split_axis=0, concat_axis=0, tiled=True)  62.9 us
    all_to_all x5, starting transfers between devices, swap(): return lax.all_to_all(x, axes, split_axis=0, concat_axis=0, tiled=True)  40.9 us
    pallas_call x4, Pallas kernels, whole_call(): pl.pallas_call(body, out_shape=out_shape, scratch_shapes=list(scratch), c...  18.2 us
    pallas_call x1, Pallas kernels, token_weights(): pl.pallas_call(attend_body, grid=(steps // several,), out_shape=pltpu.HBM...  6.88 us
  transfers between devices with their start and end apart: 5, of which 3 were waited for; matrix products, arithmetic and copies ran while one was open for 4% of the time, Pallas kernels for 7%

profile of v5, /device:TPU:1, one launch (start us, length us, event | category | flops | bytes accessed | tf_op | source)
XLA Modules:
  0.0 314.7 jit_solution(5443786771473769952)
XLA Ops:
  0.0 4.4 %shard_map.46 = bf16[32,400,128]{2,1,0:T(8,128)(2,1)} custom-call(bf16[256,2048]{1,0:T(8,128)(2,1)} %bitcast.43, bf16[256,2048]{1,0:T(8,128)(2,1)} %bitcast.44, bf16[256,2048]{1,0:T(8,128)(2,1)} %bitcast.45, s32[2,128]{1,0:T(2,128)} %bitcast.52), custom_call_target="tpu_custom_call" | custom-call | tf_op jit(solution)/shard_map/pallas_call | solution.py:144
  4.4 16.7 %all-to-all-start = ((bf16[32,400,128]{2,1,0:T(8,128)(2,1)}), bf16[32,400,128]{2,1,0:T(8,128)(2,1)S(1)}, u32[]{:S(2)}, u32[]{:S(2)}) async-start(bf16[32,400,128]{2,1,0:T(8,128)(2,1)} %shard_map.46), calls=%async_computation | async-start | bytes 6553600 | tf_op jit(solution)/shard_map/all_to_all | solution.py:317
  21.1 0.7 broadcast_compare_fusion
  21.8 145.5 %all-to-all-done.got_ref.tile_ref = bf16[32,400,128]{2,1,0:T(8,128)(2,1)S(1)} async-done(((bf16[32,400,128]{2,1,0:T(8,128)(2,1)}), bf16[32,400,128]{2,1,0:T(8,128)(2,1)S(1)}, u32[]{:S(2)}, u32[]{:S(2)}) %all-to-all-start) | async-done | bytes 3276832 | tf_op jit(solution)/shard_map/all_to_all | solution.py:317
  167.3 3.2 %shard_map.47 = bf16[32,32,128]{2,1,0:T(8,128)(2,1)} custom-call(bf16[32,400,128]{2,1,0:T(8,128)(2,1)S(1)} %all-to-all-done.got_ref.tile_ref), custom_call_target="tpu_custom_call" | custom-call | tf_op jit(solution)/shard_map/pallas_call | solution.py:213
  170.6 7.9 %all-to-all-start.1 = ((bf16[32,32,128]{2,1,0:T(8,128)(2,1)}), bf16[32,32,128]{2,1,0:T(8,128)(2,1)S(1)}, u32[]{:S(2)}, u32[]{:S(2)}) async-start(bf16[32,32,128]{2,1,0:T(8,128)(2,1)} %shard_map.47), calls=%async_computation.1 | async-start | bytes 524288 | tf_op jit(solution)/shard_map/all_to_all | solution.py:317
  178.5 2.1 slice_bitcast_fusion
  180.6 0.7 fusion.16
  181.3 0.1 copy-done.2
  181.5 3.1 fusion.31
  184.5 2.8 all-to-all-done.1.parts_ref
  187.3 0.8 shard_map.48
  188.1 4.6 %all-to-all-start.2 = ((bf16[32,32,128]{2,1,0:T(8,128)(2,1)}), bf16[32,32,128]{2,1,0:T(8,128)(2,1)S(1)}, u32[]{:S(2)}, u32[]{:S(2)}) async-start(bf16[32,32,128]{2,1,0:T(8,128)(2,1)} %shard_map.48), calls=%async_computation.2 | async-start | bytes 524288 | tf_op jit(solution)/shard_map/all_to_all | solution.py:317
  192.7 3.3 %fusion.11 = bf16[16,32,8,128]{3,2,1,0:T(8,128)(2,1)S(1)} fusion(f32[16,256,256]{1,2,0:T(8,128)} %get-tuple-element.38, f32[16,256]{1,0:T(8,128)S(1)} %get-tuple-element.37, bf16[16,32,8,128]{3,2,0,1:T(8,128)(2,1)} %get-tuple-element.29), kind=kOutput, calls=%fused_computation.15 | convolution fusion | flops 271056896 | bytes 6307840 | tf_op jit(solution)/shard_map/sab,sbe->sae/dot_general | solution.py:349
  196.0 1.3 copy.9
  197.2 4.3 %all-to-all-done.2 = bf16[32,32,128]{2,1,0:T(8,128)(2,1)S(1)} async-done(((bf16[32,32,128]{2,1,0:T(8,128)(2,1)}), bf16[32,32,128]{2,1,0:T(8,128)(2,1)S(1)}, u32[]{:S(2)}, u32[]{:S(2)}) %all-to-all-start.2) | async-done | bytes 262176 | tf_op jit(solution)/shard_map/all_to_all | solution.py:317
  201.5 0.7 fusion.30
  202.2 2.6 multiply_reduce_fusion
  204.8 0.0 copy-start
  204.8 1.5 fusion.1
  206.4 1.8 fusion.12
  208.2 0.8 copy.10
  209.1 4.3 %all-to-all-start.3 = ((bf16[32,16,256]{2,1,0:T(8,128)(2,1)}), bf16[32,16,256]{2,1,0:T(8,128)(2,1)S(1)}, u32[]{:S(2)}, u32[]{:S(2)}) async-start(bf16[32,16,256]{2,1,0:T(8,128)(2,1)} %bitcast.42), calls=%async_computation.3 | async-start | bytes 524288 | tf_op jit(solution)/shard_map/all_to_all | solution.py:317
  213.4 11.2 %shard_map.49 = (bf16[512,512]{1,0:T(8,128)(2,1)}, bf16[512,512]{1,0:T(8,128)(2,1)}, bf16[512,512]{1,0:T(8,128)(2,1)}, bf16[512,512]{1,0:T(8,128)(2,1)}) custom-call(bf16[512,128]{1,0:T(8,128)(2,1)} %bitcast.47, bf16[512,128]{1,0:T(8,128)(2,1)} %bitcast.48), custom_call_target="tpu_custom_call" | custom-call | flops 7247757312 | bytes 262144 | tf_op jit(solution)/shard_map/pallas_call | solution.py:79
  224.6 1.0 shard_map.51
  225.6 7.3 %all-to-all-start.4 = ((bf16[32,16,128]{2,1,0:T(8,128)(2,1)}), bf16[32,16,128]{2,1,0:T(8,128)(2,1)S(1)}, u32[]{:S(2)}, u32[]{:S(2)}) async-start(bf16[32,16,128]{2,1,0:T(8,128)(2,1)} %shard_map.51), calls=%async_computation.4 | async-start | bytes 262144 | tf_op jit(solution)/shard_map/all_to_all | solution.py:317
  232.9 5.2 %shard_map.50 = (bf16[512,512]{1,0:T(8,128)(2,1)}, bf16[512,512]{1,0:T(8,128)(2,1)}) custom-call(bf16[512,512]{1,0:T(8,128)(2,1)} %get-tuple-element.21.zh_ref, bf16[512,512]{1,0:T(8,128)(2,1)} %get-tuple-element.22.zl_ref, bf16[512,512]{1,0:T(8,128)(2,1)} %get-tuple-element.23.yh_ref, bf16[512,512]{1,0:T(8,128)(2,1)} %get-tuple-element.24.yl_ref), custom_call_target="tpu_custom_call" | custom-call | flops 2415919104 | bytes 2097152 | tf_op jit(solution)/shard_map/pallas_call | solution.py:79
  238.2 6.9 %shard_map.52.attend_ref = bf16[4096,512]{1,0:T(8,128)(2,1)} custom-call(bf16[32,400,128]{2,1,0:T(8,128)(2,1)S(1)} %all-to-all-done.got_ref.tile_ref, bf16[512,128]{1,0:T(8,128)(2,1)} %bitcast.49), custom_call_target="tpu_custom_call" | custom-call | flops 2147483648 | bytes 5242880 | tf_op jit(solution)/shard_map/pallas_call | solution.py:265
  245.0 0.0 all-to-all-done.4.summary_ref
  245.1 5.1 %shard_map.53 = bf16[32,128,128]{2,1,0:T(8,128)(2,1)S(1)} custom-call(bf16[512,512]{1,0:T(8,128)(2,1)} %get-tuple-element.25.high_ref, bf16[512,512]{1,0:T(8,128)(2,1)} %get-tuple-element.26.low_ref, bf16[32,16,128]{2,1,0:T(8,128)(2,1)S(1)} %all-to-all-done.4.summary_ref, bf16[4096,512]{1,0:T(8,128)(2,1)} %shard_map.52.attend_ref, bf16[4096,128]{1,0:T(8,128)(2,1)} %bitcast.39), custom_call_target="tpu_custom_call" | custom-call | tf_op jit(solution)/shard_map/pallas_call | solution.py:299
  250.1 62.9 %all_to_all.30.in_ref = bf16[32,128,128]{2,1,0:T(8,128)(2,1)S(1)} all-to-all(bf16[32,128,128]{2,1,0:T(8,128)(2,1)S(1)} %shard_map.53), channel_id=1, replica_groups=mesh['z'=16,'core'=2,'space'=16] {'z','core'}, dimensions={0} | all-to-all | bytes 2097152 | tf_op jit(solution)/shard_map/all_to_all | solution.py:317
  313.1 1.6 shard_map.54
  (12 shorter events, 0.1 us)
Async XLA Ops:
  4.4 163.0 %all-to-all-start = ((bf16[32,400,128]{2,1,0:T(8,128)(2,1)}), bf16[32,400,128]{2,1,0:T(8,128)(2,1)S(1)}, u32[]{:S(2)}, u32[]{:S(2)}) async-start(bf16[32,400,128]{2,1,0:T(8,128)(2,1)} %shard_map.46), calls=%async_computation | async-start | bytes 6553600 | tf_op jit(solution)/shard_map/all_to_all | solution.py:317
  170.6 16.8 %all-to-all-start.1 = ((bf16[32,32,128]{2,1,0:T(8,128)(2,1)}), bf16[32,32,128]{2,1,0:T(8,128)(2,1)S(1)}, u32[]{:S(2)}, u32[]{:S(2)}) async-start(bf16[32,32,128]{2,1,0:T(8,128)(2,1)} %shard_map.47), calls=%async_computation.1 | async-start | bytes 524288 | tf_op jit(solution)/shard_map/all_to_all | solution.py:317
  180.6 0.8 copy-start.2
  188.1 13.4 %all-to-all-start.2 = ((bf16[32,32,128]{2,1,0:T(8,128)(2,1)}), bf16[32,32,128]{2,1,0:T(8,128)(2,1)S(1)}, u32[]{:S(2)}, u32[]{:S(2)}) async-start(bf16[32,32,128]{2,1,0:T(8,128)(2,1)} %shard_map.48), calls=%async_computation.2 | async-start | bytes 524288 | tf_op jit(solution)/shard_map/all_to_all | solution.py:317
  202.2 2.6 copy-start.1
  204.8 1.5 copy-start
  209.1 15.5 %all-to-all-start.3 = ((bf16[32,16,256]{2,1,0:T(8,128)(2,1)}), bf16[32,16,256]{2,1,0:T(8,128)(2,1)S(1)}, u32[]{:S(2)}, u32[]{:S(2)}) async-start(bf16[32,16,256]{2,1,0:T(8,128)(2,1)} %bitcast.42), calls=%async_computation.3 | async-start | bytes 524288 | tf_op jit(solution)/shard_map/all_to_all | solution.py:317
  225.6 19.4 %all-to-all-start.4 = ((bf16[32,16,128]{2,1,0:T(8,128)(2,1)}), bf16[32,16,128]{2,1,0:T(8,128)(2,1)S(1)}, u32[]{:S(2)}, u32[]{:S(2)}) async-start(bf16[32,16,128]{2,1,0:T(8,128)(2,1)} %shard_map.51), calls=%async_computation.4 | async-start | bytes 262144 | tf_op jit(solution)/shard_map/all_to_all | solution.py:317

commit v6 on v2

--- a/solution.py
+++ b/solution.py
@@ -10,6 +10,7 @@
 HEAD_DIM = 128
 LANDMARKS = 512
 ITERS = 3
+GROUP = 256
 ACROSS = ("z", "core")
 PLANE = ("core", "space")
 SCALE = 1.0 / math.sqrt(HEAD_DIM)
@@ -23,6 +24,10 @@
     return expo / jnp.sum(expo, axis=-1, keepdims=True)
 
 
+def in_hbm(*arrays):
+    return [pltpu.with_memory_space_constraint(x, pltpu.HBM) for x in arrays]
+
+
 def halves(x):
     high = x.astype(BF16)
     return high, (x - high.astype(F32)).astype(BF16)
@@ -31,9 +36,11 @@
 def triple(left, right):
     lh, ll = left
     rh, rl = right
-    out = jnp.dot(lh, rh, preferred_element_type=F32)
-    out += jnp.dot(lh, rl, preferred_element_type=F32)
-    return out + jnp.dot(ll, rh, preferred_element_type=F32)
+    return jnp.dot(
+        jnp.concatenate([lh, lh, ll], axis=1),
+        jnp.concatenate([rh, rl, rh], axis=0),
+        preferred_element_type=F32,
+    )
 
 
 def inverse_body(q_ref, k_ref, out_ref, kh_ref, kl_ref):
@@ -106,11 +113,11 @@
     return pl.pallas_call(
         pack_body,
         grid=(width // columns,),
-        out_shape=jax.ShapeDtypeStruct((chunks, rows, HEAD_DIM), BF16),
+        out_shape=pltpu.HBM((chunks, rows, HEAD_DIM), BF16),
         in_specs=[cut, cut, cut, pl.BlockSpec((sides, part), lambda i: (0, 0))],
         out_specs=pl.BlockSpec((quad * sides, rows, HEAD_DIM), lambda i: (i, 0, 0)),
         compiler_params=pltpu.CompilerParams(vmem_limit_bytes=24 * 2**20),
-    )(queries, keys, values, groups.reshape(sides, part))
+    )(*in_hbm(queries, keys, values, groups.reshape(sides, part)))
 
 
 def unpack_body(in_ref, out_ref):
@@ -135,13 +142,94 @@
     )(x)
 
 
+def whole_call(body, out_shape, operands, megabytes, scratch=(), flops=0):
+    size = sum(x.size * x.dtype.itemsize for x in operands)
+    return pl.pallas_call(
+        body,
+        out_shape=out_shape,
+        scratch_shapes=list(scratch),
+        compiler_params=pltpu.CompilerParams(vmem_limit_bytes=megabytes * 2**20),
+        cost_estimate=pl.CostEstimate(flops=flops, bytes_accessed=size, transcendentals=0),
+    )(*operands)
+
+
+def sums_body(got_ref, out_ref, acc_ref):
+    several = got_ref.shape[0]
+    part = (got_ref.shape[1] - 16) // 3
+    plane, pair, _ = out_ref.shape
+    block = pair // 2
+    turn = pl.program_id(0)
+
+    @pl.when(turn == 0)
+    def _():
+        acc_ref[...] = jnp.zeros_like(acc_ref)
+
+    rows = lax.broadcasted_iota(jnp.int32, (LANDMARKS, part), 0)
+    onehot, rest = [], []
+    for frame in range(several):
+        ids = got_ref[frame, 3 * part : 3 * part + 16, :].astype(F32)
+        member = (ids[0:1, :] * 256.0 + ids[1:2, :]).astype(jnp.int32)
+        onehot.append((rows == member).astype(F32).astype(BF16))
+        rest.append(
+            jnp.concatenate([got_ref[frame, :part, :], got_ref[frame, part : 2 * part, :]], axis=1)
+        )
+    acc_ref[...] += jnp.dot(
+        jnp.concatenate(onehot, axis=1),
+        jnp.concatenate(rest, axis=0),
+        preferred_element_type=F32,
+    )
+
+    @pl.when(turn == pl.num_programs(0) - 1)
+    def _():
+        for side in range(2):
+            x = acc_ref[:, side * HEAD_DIM : (side + 1) * HEAD_DIM].astype(BF16)
+            out_ref[:, side * block : (side + 1) * block, :] = x.reshape(plane, block, HEAD_DIM)
+
+
+def group_sums(got, plane):
+    steps, rows, _ = got.shape
+    several = 4
+    pair = 2 * LANDMARKS // plane
+    return pl.pallas_call(
+        sums_body,
+        grid=(steps // several,),
+        out_shape=pltpu.HBM((plane, pair, HEAD_DIM), BF16),
+        in_specs=[pl.BlockSpec((several, rows, HEAD_DIM), lambda i: (i, 0, 0))],
+        out_specs=pl.BlockSpec((plane, pair, HEAD_DIM), lambda i: (0, 0, 0)),
+        scratch_shapes=[pltpu.VMEM((LANDMARKS, 2 * HEAD_DIM), F32)],
+        compiler_params=pltpu.CompilerParams(vmem_limit_bytes=12 * 2**20),
+    )(got)
+
+
+def mean_body(parts_ref, out_ref):
+    total = jnp.sum(parts_ref[...].astype(F32), axis=0, keepdims=True)
+    mean = (total / GROUP).astype(BF16)
+    out_ref[...] = jnp.broadcast_to(mean, out_ref.shape)
+
+
+def group_means(parts):
+    return whole_call(mean_body, pltpu.HBM(parts.shape, BF16), [parts], 8)
+
+
+def combine_body(parts_ref, out_ref):
+    x = parts_ref[...].astype(F32)
+    tops = x[:, :, HEAD_DIM : HEAD_DIM + 1]
+    totals = x[:, :, HEAD_DIM + 1 : HEAD_DIM + 2] + x[:, :, HEAD_DIM + 2 : HEAD_DIM + 3]
+    factor = jnp.exp(tops - jnp.max(tops, axis=0, keepdims=True))
+    weighted = jnp.sum(x[:, :, :HEAD_DIM] * factor, axis=0, keepdims=True)
+    total = jnp.sum(totals * factor, axis=0, keepdims=True)
+    out_ref[...] = jnp.broadcast_to((weighted / total).astype(BF16), out_ref.shape)
+
+
+def combine(parts):
+    plane, block, _ = parts.shape
+    return whole_call(
+        combine_body, pltpu.HBM((plane, block, HEAD_DIM), BF16), [parts], 8
+    )
+
+
 def swap(x, axes):
     return lax.all_to_all(x, axes, split_axis=0, concat_axis=0, tiled=True)
-
-
-def share(x, axes):
-    size = lax.axis_size(axes)
-    return swap(jnp.broadcast_to(x[None], (size,) + x.shape), axes)
 
 
 def local(queries, keys, values, groups):
@@ -159,19 +247,7 @@
     q = got[:, :part].reshape(tokens, HEAD_DIM)
     k = got[:, part : 2 * part].reshape(tokens, HEAD_DIM)
     v = got[:, 2 * part : 3 * part].reshape(tokens, HEAD_DIM)
-    ids = got[:, 3 * part : 3 * part + 2].astype(F32)
-    member = (ids[:, 0] * 256.0 + ids[:, 1]).astype(jnp.int32).reshape(tokens)
-
-    landmark_ids = jnp.arange(LANDMARKS, dtype=jnp.int32)
-    onehot = (member[None, :] == landmark_ids[:, None]).astype(BF16)
-    q_part = jnp.dot(onehot, q, preferred_element_type=F32).astype(BF16)
-    k_part = jnp.dot(onehot, k, preferred_element_type=F32).astype(BF16)
-    members_each = plane * tokens // LANDMARKS
-    both = jnp.concatenate(
-        [q_part.reshape(plane, block, HEAD_DIM), k_part.reshape(plane, block, HEAD_DIM)], axis=1
-    )
-    sums = jnp.sum(swap(both, PLANE).astype(F32), axis=0)
-    lands = share((sums / members_each).astype(BF16), PLANE)
+    lands = swap(group_means(swap(group_sums(got, plane), PLANE)), PLANE)
     q_land = lands[:, :block].reshape(LANDMARKS, HEAD_DIM)
     k_land = lands[:, block:].reshape(LANDMARKS, HEAD_DIM)
 
@@ -199,13 +275,8 @@
         jnp.concatenate([own_top, high, low], axis=1), ((0, 0), (0, HEAD_DIM - 3))
     )
     own = jnp.concatenate([own_sum.astype(BF16), extra], axis=1)
-    parts = swap(own.reshape(plane, block, 2 * HEAD_DIM), PLANE).astype(F32)
-    tops = parts[:, :, HEAD_DIM : HEAD_DIM + 1]
-    totals = parts[:, :, HEAD_DIM + 1 : HEAD_DIM + 2] + parts[:, :, HEAD_DIM + 2 : HEAD_DIM + 3]
-    factor = jnp.exp(tops - jnp.max(tops, axis=0))
-    weighted = jnp.sum(parts[:, :, :HEAD_DIM] * factor, axis=0)
-    summary = (weighted / jnp.sum(totals * factor, axis=0)).astype(BF16)
-    summary = share(summary, PLANE).reshape(LANDMARKS, HEAD_DIM).astype(F32)
+    parts = swap(own.reshape(plane, block, 2 * HEAD_DIM), PLANE)
+    summary = swap(combine(parts), PLANE).reshape(LANDMARKS, HEAD_DIM).astype(F32)
 
     inverse = pseudo_inverse(q_land, k_land)
     token_logits = jnp.einsum("se,me->sm", q, k_land, preferred_element_type=F32) * SCALE

time: 314 us -> 307 us (0.978)
  local copies, waits for them, and re-layouts: 10.7 us -> 3.79 us
  Pallas kernels: 16.1 us -> 22.8 us
    pallas_call x1 -> x4, Pallas kernels: 2.54 us -> 9.32 us  [the longest x1 4.35 us: pack(): pl.pallas_call(pack_body, grid=(width // columns,), out_shape=pltpu.HBM((...]
    unnamed x22 -> x8, local copies, waits for them, and re-layouts: 4.38 us -> 0.14 us
    all_to_all x5, waiting for transfers between devices: 160 us -> 157 us  [swap(): return lax.all_to_all(x, axes, split_axis=0, concat_axis=0, tiled=True)]
  transfers between devices with their start and end apart: 5 -> 5, of which waited for: 4 -> 4; matrix products, arithmetic and copies ran while one was open for 4% -> 5% of each run, Pallas kernels for 4% -> 4%
where the time goes in v6:
time: 307 us
  waiting for transfers between devices  157 us (51%)
  blocking collectives  63 us (21%)
  starting transfers between devices  38.2 us (12%)
  Pallas kernels  22.8 us (7%)
  matrix products  12.4 us (4%)
  other arithmetic  9.69 us (3%)
  local copies, waits for them, and re-layouts  3.79 us (1%)
    all_to_all x5, waiting for transfers between devices, swap(): return lax.all_to_all(x, axes, split_axis=0, concat_axis=0, tiled=True)  157 us
    all_to_all x1, blocking collectives, swap(): return lax.all_to_all(x, axes, split_axis=0, concat_axis=0, tiled=True)  63 us
    all_to_all x5, starting transfers between devices, swap(): return lax.all_to_all(x, axes, split_axis=0, concat_axis=0, tiled=True)  38.2 us
    pallas_call x1, Pallas kernels, pseudo_inverse(): pl.pallas_call(inverse_body, out_shape=jax.ShapeDtypeStruct((LANDMARKS, L...  11.9 us
  transfers between devices with their start and end apart: 5, of which 4 were waited for; matrix products, arithmetic and copies ran while one was open for 5% of the time, Pallas kernels for 4%

profile of v6, /device:TPU:1, one launch (start us, length us, event | category | flops | bytes accessed | tf_op | source)
XLA Modules:
  0.0 306.5 jit_solution(6649487471139145307)
XLA Ops:
  0.0 4.3 %shard_map.46 = bf16[32,400,128]{2,1,0:T(8,128)(2,1)} custom-call(bf16[256,2048]{1,0:T(8,128)(2,1)} %bitcast.57, bf16[256,2048]{1,0:T(8,128)(2,1)} %bitcast.58, bf16[256,2048]{1,0:T(8,128)(2,1)} %bitcast.59, s32[2,128]{1,0:T(2,128)} %bitcast.63), custom_call_target="tpu_custom_call" | custom-call | tf_op jit(solution)/shard_map/pallas_call | solution.py:113
  4.3 16.7 %all-to-all-start = ((bf16[32,400,128]{2,1,0:T(8,128)(2,1)}), bf16[32,400,128]{2,1,0:T(8,128)(2,1)S(1)}, u32[]{:S(2)}, u32[]{:S(2)}) async-start(bf16[32,400,128]{2,1,0:T(8,128)(2,1)} %shard_map.46), calls=%async_computation | async-start | bytes 6553600 | tf_op jit(solution)/shard_map/all_to_all | solution.py:232
  21.1 0.7 broadcast_compare_fusion
  21.8 145.5 %all-to-all-done.got_ref = bf16[32,400,128]{2,1,0:T(8,128)(2,1)S(1)} async-done(((bf16[32,400,128]{2,1,0:T(8,128)(2,1)}), bf16[32,400,128]{2,1,0:T(8,128)(2,1)S(1)}, u32[]{:S(2)}, u32[]{:S(2)}) %all-to-all-start) | async-done | bytes 3276832 | tf_op jit(solution)/shard_map/all_to_all | solution.py:232
  167.3 3.2 %shard_map.47 = bf16[32,32,128]{2,1,0:T(8,128)(2,1)} custom-call(bf16[32,400,128]{2,1,0:T(8,128)(2,1)S(1)} %all-to-all-done.got_ref), custom_call_target="tpu_custom_call" | custom-call | tf_op jit(solution)/shard_map/pallas_call | solution.py:193
  170.5 8.0 %all-to-all-start.1 = ((bf16[32,32,128]{2,1,0:T(8,128)(2,1)}), bf16[32,32,128]{2,1,0:T(8,128)(2,1)S(1)}, u32[]{:S(2)}, u32[]{:S(2)}) async-start(bf16[32,32,128]{2,1,0:T(8,128)(2,1)} %shard_map.47), calls=%async_computation.1 | async-start | bytes 524288 | tf_op jit(solution)/shard_map/all_to_all | solution.py:232
  178.5 2.5 slice_bitcast_fusion
  181.0 0.7 fusion.18
  181.7 0.1 copy-done.3
  181.9 3.1 fusion.33
  184.9 2.4 all-to-all-done.1.parts_ref
  187.3 0.8 shard_map.48
  188.1 5.0 %all-to-all-start.2 = ((bf16[32,32,128]{2,1,0:T(8,128)(2,1)}), bf16[32,32,128]{2,1,0:T(8,128)(2,1)S(1)}, u32[]{:S(2)}, u32[]{:S(2)}) async-start(bf16[32,32,128]{2,1,0:T(8,128)(2,1)} %shard_map.48), calls=%async_computation.2 | async-start | bytes 524288 | tf_op jit(solution)/shard_map/all_to_all | solution.py:232
  193.1 3.1 %fusion.13 = bf16[32,16,8,128]{3,2,0,1:T(8,128)(2,1)S(1)} fusion(f32[16,256,256]{1,2,0:T(8,128)} %get-tuple-element.17, f32[16,256]{1,0:T(8,128)S(1)} %get-tuple-element.16, bf16[16,32,8,128]{3,2,0,1:T(8,128)(2,1)S(1)} %copy-done.2), kind=kOutput, calls=%fused_computation.21 | convolution fusion | flops 271056896 | bytes 6307840 | tf_op jit(solution)/shard_map/sab,sbe->sae/dot_general | solution.py:264
  196.2 0.3 copy.9
  196.5 5.4 %all-to-all-done.2 = bf16[32,32,128]{2,1,0:T(8,128)(2,1)S(1)} async-done(((bf16[32,32,128]{2,1,0:T(8,128)(2,1)}), bf16[32,32,128]{2,1,0:T(8,128)(2,1)S(1)}, u32[]{:S(2)}, u32[]{:S(2)}) %all-to-all-start.2) | async-done | bytes 262176 | tf_op jit(solution)/shard_map/all_to_all | solution.py:232
  201.9 1.3 multiply_reduce_fusion
  203.3 1.5 fusion.2
  204.8 1.8 fusion.14
  206.7 0.8 copy.10
  207.6 4.3 %all-to-all-start.3 = ((bf16[32,16,256]{2,1,0:T(8,128)(2,1)}), bf16[32,16,256]{2,1,0:T(8,128)(2,1)S(1)}, u32[]{:S(2)}, u32[]{:S(2)}) async-start(bf16[32,16,256]{2,1,0:T(8,128)(2,1)} %bitcast.21), calls=%async_computation.3 | async-start | bytes 524288 | tf_op jit(solution)/shard_map/all_to_all | solution.py:232
  211.9 1.3 multiply_reduce_fusion.1
  213.1 1.4 fusion.1
  214.5 3.0 divide_convert_fusion
  217.5 3.2 %all-to-all-done.3.parts_ref = bf16[32,16,256]{2,1,0:T(8,128)(2,1)S(1)} async-done(((bf16[32,16,256]{2,1,0:T(8,128)(2,1)}), bf16[32,16,256]{2,1,0:T(8,128)(2,1)S(1)}, u32[]{:S(2)}, u32[]{:S(2)}) %all-to-all-start.3) | async-done | bytes 262176 | tf_op jit(solution)/shard_map/all_to_all | solution.py:232
  220.7 1.0 shard_map.50
  221.7 4.3 %all-to-all-start.4 = ((bf16[32,16,128]{2,1,0:T(8,128)(2,1)}), bf16[32,16,128]{2,1,0:T(8,128)(2,1)S(1)}, u32[]{:S(2)}, u32[]{:S(2)}) async-start(bf16[32,16,128]{2,1,0:T(8,128)(2,1)} %shard_map.50), calls=%async_computation.4 | async-start | bytes 262144 | tf_op jit(solution)/shard_map/all_to_all | solution.py:232
  226.0 11.9 %shard_map.49 = f32[512,512]{1,0:T(8,128)S(1)} custom-call(bf16[512,128]{1,0:T(8,128)(2,1)S(1)} %bitcast.49, bf16[512,128]{1,0:T(8,128)(2,1)S(1)} %bitcast.51), custom_call_target="tpu_custom_call" | custom-call | flops 9663676416 | bytes 2097152 | tf_op jit(solution)/shard_map/pallas_call | solution.py:72
  237.9 0.6 convolution_convert_fusion
  238.5 3.5 %fusion.4 = bf16[4096,128]{1,0:T(8,128)(2,1)S(1)} fusion(bf16[4096,512]{0,1:T(8,128)(2,1)} %divide_convert_fusion, bf16[512,128]{1,0:T(8,128)(2,1)S(1)} %convolution_convert_fusion, bf16[4096,128]{1,0:T(8,128)(2,1)S(1)} %bitcast.53), kind=kOutput, calls=%fused_computation.10 | convolution fusion | flops 538443776 | bytes 6422528 | tf_op jit(solution)/shard_map/dot_general | solution.py:285
  242.0 63.0 %all_to_all.30.in_ref = bf16[32,128,128]{2,1,0:T(8,128)(2,1)S(1)} all-to-all(bf16[32,128,128]{2,1,0:T(8,128)(2,1)S(1)} %bitcast.54), channel_id=1, replica_groups=mesh['z'=16,'core'=2,'space'=16] {'z','core'}, dimensions={0} | all-to-all | bytes 2097152 | tf_op jit(solution)/shard_map/all_to_all | solution.py:232
  304.9 1.6 shard_map.51
  (16 shorter events, 0.1 us)
Async XLA Ops:
  4.3 163.0 %all-to-all-start = ((bf16[32,400,128]{2,1,0:T(8,128)(2,1)}), bf16[32,400,128]{2,1,0:T(8,128)(2,1)S(1)}, u32[]{:S(2)}, u32[]{:S(2)}) async-start(bf16[32,400,128]{2,1,0:T(8,128)(2,1)} %shard_map.46), calls=%async_computation | async-start | bytes 6553600 | tf_op jit(solution)/shard_map/all_to_all | solution.py:232
  170.5 16.8 %all-to-all-start.1 = ((bf16[32,32,128]{2,1,0:T(8,128)(2,1)}), bf16[32,32,128]{2,1,0:T(8,128)(2,1)S(1)}, u32[]{:S(2)}, u32[]{:S(2)}) async-start(bf16[32,32,128]{2,1,0:T(8,128)(2,1)} %shard_map.47), calls=%async_computation.1 | async-start | bytes 524288 | tf_op jit(solution)/shard_map/all_to_all | solution.py:232
  181.0 0.8 copy-start.3
  181.9 11.2 %copy-start.2 = (bf16[16,32,8,128]{3,2,0,1:T(8,128)(2,1)S(1)}, bf16[16,32,8,128]{3,2,0,1:T(8,128)(2,1)}, u32[]{:S(2)}) copy-start(bf16[16,32,8,128]{3,2,0,1:T(8,128)(2,1)} %get-tuple-element.5) | copy-start | bytes 3145732
  188.1 13.8 %all-to-all-start.2 = ((bf16[32,32,128]{2,1,0:T(8,128)(2,1)}), bf16[32,32,128]{2,1,0:T(8,128)(2,1)S(1)}, u32[]{:S(2)}, u32[]{:S(2)}) async-start(bf16[32,32,128]{2,1,0:T(8,128)(2,1)} %shard_map.48), calls=%async_computation.2 | async-start | bytes 524288 | tf_op jit(solution)/shard_map/all_to_all | solution.py:232
  193.1 8.8 %copy-start.1 = (bf16[32,128,128]{2,1,0:T(8,128)(2,1)S(1)}, bf16[32,128,128]{2,1,0:T(8,128)(2,1)}, u32[]{:S(2)}) copy-start(bf16[32,128,128]{2,1,0:T(8,128)(2,1)} %get-tuple-element.8) | copy-start | bytes 3145732
  204.8 7.1 %copy-start = (bf16[32,128,128]{2,1,0:T(8,128)(2,1)S(1)}, bf16[32,128,128]{2,1,0:T(8,128)(2,1)}, u32[]{:S(2)}) copy-start(bf16[32,128,128]{2,1,0:T(8,128)(2,1)} %get-tuple-element.9) | copy-start | bytes 3145732
  207.6 13.1 %all-to-all-start.3 = ((bf16[32,16,256]{2,1,0:T(8,128)(2,1)}), bf16[32,16,256]{2,1,0:T(8,128)(2,1)S(1)}, u32[]{:S(2)}, u32[]{:S(2)}) async-start(bf16[32,16,256]{2,1,0:T(8,128)(2,1)} %bitcast.21), calls=%async_computation.3 | async-start | bytes 524288 | tf_op jit(solution)/shard_map/all_to_all | solution.py:232
  221.7 16.2 %all-to-all-start.4 = ((bf16[32,16,128]{2,1,0:T(8,128)(2,1)}), bf16[32,16,128]{2,1,0:T(8,128)(2,1)S(1)}, u32[]{:S(2)}, u32[]{:S(2)}) async-start(bf16[32,16,128]{2,1,0:T(8,128)(2,1)} %shard_map.50), calls=%async_computation.4 | async-start | bytes 262144 | tf_op jit(solution)/shard_map/all_to_all | solution.py:232

commit v7 on v6

--- a/solution.py
+++ b/solution.py
@@ -11,6 +11,7 @@
 LANDMARKS = 512
 ITERS = 3
 GROUP = 256
+EXTRA = 8
 ACROSS = ("z", "core")
 PLANE = ("core", "space")
 SCALE = 1.0 / math.sqrt(HEAD_DIM)
@@ -85,7 +86,7 @@
 def pack_body(q_ref, k_ref, v_ref, id_ref, out_ref):
     sides, part = id_ref.shape
     quad = out_ref.shape[0] // sides
-    row = lax.broadcasted_iota(jnp.int32, (16, part), 0)
+    row = lax.broadcasted_iota(jnp.int32, (EXTRA, part), 0)
     for side in range(sides):
         ids = id_ref[side : side + 1, :]
         coarse = lax.shift_right_logical(ids, 8)
@@ -99,16 +100,16 @@
             out_ref[chunk, :part, :] = q_ref[rows, lanes]
             out_ref[chunk, part : 2 * part, :] = k_ref[rows, lanes]
             out_ref[chunk, 2 * part : 3 * part, :] = v_ref[rows, lanes]
-            out_ref[chunk, 3 * part : 3 * part + 16, :] = tile
+            out_ref[chunk, 3 * part : 3 * part + EXTRA, :] = tile
 
 
 def pack(queries, keys, values, groups, sides):
     count, width = queries.shape
     part = count // sides
-    quad = 4
+    quad = 2
     columns = quad * HEAD_DIM
     cut = pl.BlockSpec((count, columns), lambda i: (0, i))
-    rows = 3 * part + 16
+    rows = 3 * part + EXTRA
     chunks = width // HEAD_DIM * sides
     return pl.pallas_call(
         pack_body,
@@ -131,7 +132,7 @@
 
 def unpack(x, sides):
     chunks, part, _ = x.shape
-    quad = 4
+    quad = 2
     return pl.pallas_call(
         unpack_body,
         grid=(chunks // sides // quad,),
@@ -155,7 +156,7 @@
 
 def sums_body(got_ref, out_ref, acc_ref):
     several = got_ref.shape[0]
-    part = (got_ref.shape[1] - 16) // 3
+    part = (got_ref.shape[1] - EXTRA) // 3
     plane, pair, _ = out_ref.shape
     block = pair // 2
     turn = pl.program_id(0)
@@ -167,7 +168,7 @@
     rows = lax.broadcasted_iota(jnp.int32, (LANDMARKS, part), 0)
     onehot, rest = [], []
     for frame in range(several):
-        ids = got_ref[frame, 3 * part : 3 * part + 16, :].astype(F32)
+        ids = got_ref[frame, 3 * part : 3 * part + EXTRA, :].astype(F32)
         member = (ids[0:1, :] * 256.0 + ids[1:2, :]).astype(jnp.int32)
         onehot.append((rows == member).astype(F32).astype(BF16))
         rest.append(

time: 307 us -> 308 us (level)
  Pallas kernels: 22.8 us -> 26.1 us
where the time goes in v7:
time: 308 us; the launch traced here: 307 us
  waiting for transfers between devices  155 us (50%)
  blocking collectives  62.8 us (20%)
  starting transfers between devices  38.2 us (12%)
  Pallas kernels  26.1 us (8%)
  matrix products  12.4 us (4%)
  other arithmetic  9.16 us (3%)
  local copies, waits for them, and re-layouts  3.67 us (1%)
    all_to_all x5, waiting for transfers between devices, swap(): return lax.all_to_all(x, axes, split_axis=0, concat_axis=0, tiled=True)  155 us
    all_to_all x1, blocking collectives, swap(): return lax.all_to_all(x, axes, split_axis=0, concat_axis=0, tiled=True)  62.8 us
    all_to_all x5, starting transfers between devices, swap(): return lax.all_to_all(x, axes, split_axis=0, concat_axis=0, tiled=True)  38.2 us
    pallas_call x1, Pallas kernels, pseudo_inverse(): pl.pallas_call(inverse_body, out_shape=jax.ShapeDtypeStruct((LANDMARKS, L...  11.9 us
    pallas_call x1, Pallas kernels, pack(): pl.pallas_call(pack_body, grid=(width // columns,), out_shape=pltpu.HBM((...  6.46 us
  transfers between devices with their start and end apart: 5, of which 4 were waited for; matrix products, arithmetic and copies ran while one was open for 5% of the time, Pallas kernels for 4%

profile of v7, /device:TPU:1, one launch (start us, length us, event | category | flops | bytes accessed | tf_op | source)
XLA Modules:
  0.0 306.9 jit_solution(14255988492349726578)
XLA Ops:
  0.0 6.5 %shard_map.46 = bf16[32,392,128]{2,1,0:T(8,128)(2,1)} custom-call(bf16[256,2048]{1,0:T(8,128)(2,1)} %bitcast.57, bf16[256,2048]{1,0:T(8,128)(2,1)} %bitcast.58, bf16[256,2048]{1,0:T(8,128)(2,1)} %bitcast.59, s32[2,128]{1,0:T(2,128)} %bitcast.63), custom_call_target="tpu_custom_call" | custom-call | tf_op jit(solution)/shard_map/pallas_call | solution.py:114
  6.5 16.7 %all-to-all-start = ((bf16[32,392,128]{2,1,0:T(8,128)(2,1)}), bf16[32,392,128]{2,1,0:T(8,128)(2,1)S(1)}, u32[]{:S(2)}, u32[]{:S(2)}) async-start(bf16[32,392,128]{2,1,0:T(8,128)(2,1)} %shard_map.46), calls=%async_computation | async-start | bytes 6422528 | tf_op jit(solution)/shard_map/all_to_all | solution.py:233
  23.2 0.1 broadcast_compare_fusion
  23.3 143.5 %all-to-all-done.got_ref = bf16[32,392,128]{2,1,0:T(8,128)(2,1)S(1)} async-done(((bf16[32,392,128]{2,1,0:T(8,128)(2,1)}), bf16[32,392,128]{2,1,0:T(8,128)(2,1)S(1)}, u32[]{:S(2)}, u32[]{:S(2)}) %all-to-all-start) | async-done | bytes 3211296 | tf_op jit(solution)/shard_map/all_to_all | solution.py:233
  166.8 3.2 %shard_map.47 = bf16[32,32,128]{2,1,0:T(8,128)(2,1)} custom-call(bf16[32,392,128]{2,1,0:T(8,128)(2,1)S(1)} %all-to-all-done.got_ref), custom_call_target="tpu_custom_call" | custom-call | tf_op jit(solution)/shard_map/pallas_call | solution.py:194
  170.0 8.0 %all-to-all-start.1 = ((bf16[32,32,128]{2,1,0:T(8,128)(2,1)}), bf16[32,32,128]{2,1,0:T(8,128)(2,1)S(1)}, u32[]{:S(2)}, u32[]{:S(2)}) async-start(bf16[32,32,128]{2,1,0:T(8,128)(2,1)} %shard_map.47), calls=%async_computation.1 | async-start | bytes 524288 | tf_op jit(solution)/shard_map/all_to_all | solution.py:233
  178.0 2.5 slice_bitcast_fusion
  180.5 0.7 fusion.18
  181.2 0.0 copy-start.2
  181.2 3.1 fusion.33
  184.3 2.5 all-to-all-done.1.parts_ref
  186.8 0.8 shard_map.48
  187.6 4.8 %all-to-all-start.2 = ((bf16[32,32,128]{2,1,0:T(8,128)(2,1)}), bf16[32,32,128]{2,1,0:T(8,128)(2,1)S(1)}, u32[]{:S(2)}, u32[]{:S(2)}) async-start(bf16[32,32,128]{2,1,0:T(8,128)(2,1)} %shard_map.48), calls=%async_computation.2 | async-start | bytes 524288 | tf_op jit(solution)/shard_map/all_to_all | solution.py:233
  192.5 3.1 %fusion.13 = bf16[32,16,8,128]{3,2,0,1:T(8,128)(2,1)S(1)} fusion(f32[16,256,256]{1,2,0:T(8,128)} %get-tuple-element.17, f32[16,256]{1,0:T(8,128)S(1)} %get-tuple-element.16, bf16[16,32,8,128]{3,2,0,1:T(8,128)(2,1)S(1)} %copy-done.2), kind=kOutput, calls=%fused_computation.21 | convolution fusion | flops 271056896 | bytes 6307840 | tf_op jit(solution)/shard_map/sab,sbe->sae/dot_general | solution.py:265
  195.6 0.3 copy.9
  195.9 5.4 %all-to-all-done.2 = bf16[32,32,128]{2,1,0:T(8,128)(2,1)S(1)} async-done(((bf16[32,32,128]{2,1,0:T(8,128)(2,1)}), bf16[32,32,128]{2,1,0:T(8,128)(2,1)S(1)}, u32[]{:S(2)}, u32[]{:S(2)}) %all-to-all-start.2) | async-done | bytes 262176 | tf_op jit(solution)/shard_map/all_to_all | solution.py:233
  201.3 1.3 multiply_reduce_fusion
  202.7 1.5 fusion.2
  204.2 1.9 fusion.14
  206.1 0.8 copy.10
  207.0 4.3 %all-to-all-start.3 = ((bf16[32,16,256]{2,1,0:T(8,128)(2,1)}), bf16[32,16,256]{2,1,0:T(8,128)(2,1)S(1)}, u32[]{:S(2)}, u32[]{:S(2)}) async-start(bf16[32,16,256]{2,1,0:T(8,128)(2,1)} %bitcast.21), calls=%async_computation.3 | async-start | bytes 524288 | tf_op jit(solution)/shard_map/all_to_all | solution.py:233
  211.3 1.3 multiply_reduce_fusion.1
  212.5 1.4 fusion.1
  213.9 3.0 divide_convert_fusion
  217.0 3.1 %all-to-all-done.3.parts_ref = bf16[32,16,256]{2,1,0:T(8,128)(2,1)S(1)} async-done(((bf16[32,16,256]{2,1,0:T(8,128)(2,1)}), bf16[32,16,256]{2,1,0:T(8,128)(2,1)S(1)}, u32[]{:S(2)}, u32[]{:S(2)}) %all-to-all-start.3) | async-done | bytes 262176 | tf_op jit(solution)/shard_map/all_to_all | solution.py:233
  220.1 1.0 shard_map.50
  221.1 4.3 %all-to-all-start.4 = ((bf16[32,16,128]{2,1,0:T(8,128)(2,1)}), bf16[32,16,128]{2,1,0:T(8,128)(2,1)S(1)}, u32[]{:S(2)}, u32[]{:S(2)}) async-start(bf16[32,16,128]{2,1,0:T(8,128)(2,1)} %shard_map.50), calls=%async_computation.4 | async-start | bytes 262144 | tf_op jit(solution)/shard_map/all_to_all | solution.py:233
  225.4 11.9 %shard_map.49 = f32[512,512]{1,0:T(8,128)S(1)} custom-call(bf16[512,128]{1,0:T(8,128)(2,1)S(1)} %bitcast.49, bf16[512,128]{1,0:T(8,128)(2,1)S(1)} %bitcast.51), custom_call_target="tpu_custom_call" | custom-call | flops 9663676416 | bytes 2097152 | tf_op jit(solution)/shard_map/pallas_call | solution.py:73
  237.3 0.6 convolution_convert_fusion
  237.9 3.5 %fusion.4 = bf16[4096,128]{1,0:T(8,128)(2,1)S(1)} fusion(bf16[4096,512]{0,1:T(8,128)(2,1)} %divide_convert_fusion, bf16[512,128]{1,0:T(8,128)(2,1)S(1)} %convolution_convert_fusion, bf16[4096,128]{1,0:T(8,128)(2,1)S(1)} %bitcast.53), kind=kOutput, calls=%fused_computation.10 | convolution fusion | flops 538443776 | bytes 6422528 | tf_op jit(solution)/shard_map/dot_general | solution.py:286
  241.4 62.8 %all_to_all.30.in_ref = bf16[32,128,128]{2,1,0:T(8,128)(2,1)S(1)} all-to-all(bf16[32,128,128]{2,1,0:T(8,128)(2,1)S(1)} %bitcast.54), channel_id=1, replica_groups=mesh['z'=16,'core'=2,'space'=16] {'z','core'}, dimensions={0} | all-to-all | bytes 2097152 | tf_op jit(solution)/shard_map/all_to_all | solution.py:233
  304.2 2.7 shard_map.51
  (14 shorter events, 0.1 us)
Async XLA Ops:
  6.5 160.3 %all-to-all-start = ((bf16[32,392,128]{2,1,0:T(8,128)(2,1)}), bf16[32,392,128]{2,1,0:T(8,128)(2,1)S(1)}, u32[]{:S(2)}, u32[]{:S(2)}) async-start(bf16[32,392,128]{2,1,0:T(8,128)(2,1)} %shard_map.46), calls=%async_computation | async-start | bytes 6422528 | tf_op jit(solution)/shard_map/all_to_all | solution.py:233
  170.0 16.8 %all-to-all-start.1 = ((bf16[32,32,128]{2,1,0:T(8,128)(2,1)}), bf16[32,32,128]{2,1,0:T(8,128)(2,1)S(1)}, u32[]{:S(2)}, u32[]{:S(2)}) async-start(bf16[32,32,128]{2,1,0:T(8,128)(2,1)} %shard_map.47), calls=%async_computation.1 | async-start | bytes 524288 | tf_op jit(solution)/shard_map/all_to_all | solution.py:233
  181.2 11.2 %copy-start.2 = (bf16[16,32,8,128]{3,2,0,1:T(8,128)(2,1)S(1)}, bf16[16,32,8,128]{3,2,0,1:T(8,128)(2,1)}, u32[]{:S(2)}) copy-start(bf16[16,32,8,128]{3,2,0,1:T(8,128)(2,1)} %get-tuple-element.5) | copy-start | bytes 3145732
  187.6 13.7 %all-to-all-start.2 = ((bf16[32,32,128]{2,1,0:T(8,128)(2,1)}), bf16[32,32,128]{2,1,0:T(8,128)(2,1)S(1)}, u32[]{:S(2)}, u32[]{:S(2)}) async-start(bf16[32,32,128]{2,1,0:T(8,128)(2,1)} %shard_map.48), calls=%async_computation.2 | async-start | bytes 524288 | tf_op jit(solution)/shard_map/all_to_all | solution.py:233
  192.5 8.8 %copy-start.1 = (bf16[32,128,128]{2,1,0:T(8,128)(2,1)S(1)}, bf16[32,128,128]{2,1,0:T(8,128)(2,1)}, u32[]{:S(2)}) copy-start(bf16[32,128,128]{2,1,0:T(8,128)(2,1)} %get-tuple-element.8) | copy-start | bytes 3145732
  204.2 7.1 %copy-start = (bf16[32,128,128]{2,1,0:T(8,128)(2,1)S(1)}, bf16[32,128,128]{2,1,0:T(8,128)(2,1)}, u32[]{:S(2)}) copy-start(bf16[32,128,128]{2,1,0:T(8,128)(2,1)} %get-tuple-element.9) | copy-start | bytes 3145732
  207.0 13.1 %all-to-all-start.3 = ((bf16[32,16,256]{2,1,0:T(8,128)(2,1)}), bf16[32,16,256]{2,1,0:T(8,128)(2,1)S(1)}, u32[]{:S(2)}, u32[]{:S(2)}) async-start(bf16[32,16,256]{2,1,0:T(8,128)(2,1)} %bitcast.21), calls=%async_computation.3 | async-start | bytes 524288 | tf_op jit(solution)/shard_map/all_to_all | solution.py:233
  221.1 16.2 %all-to-all-start.4 = ((bf16[32,16,128]{2,1,0:T(8,128)(2,1)}), bf16[32,16,128]{2,1,0:T(8,128)(2,1)S(1)}, u32[]{:S(2)}, u32[]{:S(2)}) async-start(bf16[32,16,128]{2,1,0:T(8,128)(2,1)} %shard_map.50), calls=%async_computation.4 | async-start | bytes 262144 | tf_op jit(solution)/shard_map/all_to_all | solution.py:233
